TPU v7x, 512 devices: a whole 4x8x8 slice. The times are simulated.
512 devices in a mesh: seq: 128 (over y, z, core), head: 4 (over x).
Axes of the slice: x: 4, y: 8, z: 8, core: 2. Of those that a mesh axis runs over, the one named last changes fastest.
Arguments:
- queries: bfloat16 [32768, 1024], P('seq', 'head'), may hold values from -5 to 5
- keys: bfloat16 [32768, 1024], P('seq', 'head'), may hold values from -5 to 5
- values: bfloat16 [32768, 1024], P('seq', 'head'), may hold values from -6 to 6
- out_grad: bfloat16 [32768, 1024], P('seq', 'head'), may hold values from -6 to 6
- sorted_position: int32 [2, 32768], P(None, ('seq', 'head')), may hold values from 0 to 32767, as said below
Outputs:
- query_grad: bfloat16 [32768, 1024], P('seq', 'head')
- key_grad: bfloat16 [32768, 1024], P('seq', 'head')
- value_grad: bfloat16 [32768, 1024], P('seq', 'head')
Inputs may be any that keep to these rules, and one draw needn't show every extreme that they name: `sorted_position`: each row is a permutation of 0 to 32767. For every round, at most 4 tokens of one block of 256 consecutive tokens take places in one block of 256 consecutive places, and every block of places takes exactly 4 from some block of tokens.
All inputs are finite; a program needn't handle non-finite values.
Results may differ from a plain program's by a relative error of at most 0.025.
Values may be sent and summed in bfloat16 or wider, within the bound.
No kernel may reach another device: no remote copies, remote signals or barrier semaphores. Data moves between devices by JAX's collectives and lax.ppermute only.
A program may use at most 64 MiB of HBM per device.

v0:
```python
import functools
import math

import jax
import jax.numpy as jnp
from jax import lax
from jax.experimental import pallas as pl
from jax.experimental.pallas import tpu as pltpu
from jax.sharding import PartitionSpec as P

HEAD_DIM = 128
SPAN = 256
ROUNDS = 2
CAP = 4
SLOTS = ROUNDS * CAP
LANES = 128
EMPTY = 8.0
SCALE = 1.0 / math.sqrt(HEAD_DIM)
F32 = jnp.float32
BF16 = jnp.bfloat16
I32 = jnp.int32


def iota(shape, dim):
    return lax.broadcasted_iota(I32, shape, dim)


def hot(condition):
    return jnp.where(condition, 1.0, 0.0).astype(BF16)


def dot(a, b):
    return lax.dot_general(a, b, (((1,), (0,)), ((), ())), preferred_element_type=F32)


def dot_nt(a, b):
    return lax.dot_general(a, b, (((1,), (1,)), ((), ())), preferred_element_type=F32)


def dot_tn(a, b):
    return lax.dot_general(a, b, (((0,), (0,)), ((), ())), preferred_element_type=F32)


def three_parts(x):
    high = x.astype(BF16).astype(F32)
    rest = x - high
    middle = rest.astype(BF16).astype(F32)
    return high, middle, (rest - middle).astype(BF16).astype(F32)


def picked(x, onehot, product):
    rows = x.shape[0]
    stacked = jnp.concatenate(three_parts(x), axis=0).astype(BF16)
    out = product(stacked, onehot)
    return out[:rows] + out[rows : 2 * rows] + out[2 * rows :]


def slot_rows(slots_ref, turn):
    slot = slots_ref[turn : turn + 1, :]
    return slot >> 3, slot & 7


def compaction(valid, n):
    before = hot(iota((LANES, LANES), 0) < iota((LANES, LANES), 1))
    lane = iota((8, LANES), 1)
    turn = iota((8, LANES), 0)
    running = jnp.zeros((8, 1), F32)
    pieces = []
    for chunk in range(n * SLOTS // LANES):
        part = valid[:, chunk * LANES : (chunk + 1) * LANES]
        mine = jnp.where((((lane >> 2) & 1) == turn) & part, 1.0, 0.0)
        rank = dot(mine.astype(BF16), before) + running
        running = running + jnp.sum(mine, axis=1, keepdims=True)
        place = jnp.where(mine > 0.0, rank.astype(I32) + turn * SPAN + 1, 0)
        pieces.append(jnp.sum(place, axis=0, keepdims=True) - 1)
    return jnp.concatenate(pieces, axis=1)


def to_slot_lanes(table, groups, n):
    rows = groups * SLOTS
    flat = n * SLOTS
    owner = hot((iota((n, flat), 1) >> 3) == iota((n, flat), 0))
    spread = picked(jnp.transpose(table)[:rows], owner, dot)
    keep = (iota((SLOTS, flat), 1) & 7) == iota((SLOTS, flat), 0)
    return [
        jnp.sum(jnp.where(keep, spread[g * SLOTS : (g + 1) * SLOTS], 0.0), axis=0, keepdims=True)
        for g in range(groups)
    ]


def pack_kernel(n, pos_ref, q_ref, g_ref, k_ref, v_ref, send_ref, slots_ref):
    tokens = q_ref.shape[0]
    width = q_ref.shape[1]
    quarters = pos_ref.shape[0] // ROUNDS
    before = hot(iota((tokens, tokens), 0) < iota((tokens, tokens), 1))
    rows = []
    for turn in range(ROUNDS):
        places = jnp.concatenate(
            [pos_ref[x * ROUNDS + turn : x * ROUNDS + turn + 1, :] for x in range(quarters)], axis=1
        )
        target = places >> 8
        member = iota((n, tokens), 0) == target
        earlier = dot(hot(member), before)
        rank = jnp.sum(jnp.where(member, earlier, 0.0), axis=0, keepdims=True).astype(I32)
        rows.append(target * SLOTS + turn * CAP + rank)
    slots_ref[...] = jnp.concatenate(rows + [jnp.zeros((8 - ROUNDS, tokens), I32)], axis=0)
    at = iota((n * SLOTS, tokens), 0)
    chosen = hot((at == rows[0]) | (at == rows[1]))
    filled = dot(chosen, jnp.ones((tokens, LANES), BF16))
    mark = jnp.where(iota((n * SLOTS, LANES), 1) == 0, EMPTY * (1.0 - filled), 0.0)
    first = dot(chosen, q_ref[...])
    send_ref[:, :LANES] = (first[:, :LANES] + mark).astype(BF16)
    send_ref[:, LANES:width] = first[:, LANES:].astype(BF16)
    for at_unit, ref in enumerate((g_ref, k_ref, v_ref)):
        send_ref[:, (at_unit + 1) * width : (at_unit + 2) * width] = dot(chosen, ref[...]).astype(BF16)


def unpack_kernel(n, recv_ref, qg_ref, kv_ref, code_ref):
    half = qg_ref.shape[1]
    flat = n * SLOTS
    lead = hot(iota((8, LANES), 1) == 0)
    first = dot_nt(lead, recv_ref[:, :LANES])
    code = compaction(first < EMPTY - 1.0, n)
    code_ref[...] = jnp.broadcast_to(code, code_ref.shape)
    chosen = hot(iota((ROUNDS * SPAN, flat), 0) == code)
    qg_ref[...] = dot(chosen, recv_ref[:, :half]).astype(BF16)
    kv_ref[...] = dot(chosen, recv_ref[:, half:]).astype(BF16)


def blocks(ref, turn, head, heads):
    rows = slice(turn * SPAN, (turn + 1) * SPAN)
    width = heads * HEAD_DIM
    lower = slice(head * HEAD_DIM, (head + 1) * HEAD_DIM)
    upper = slice(width + head * HEAD_DIM, width + (head + 1) * HEAD_DIM)
    return ref[rows, lower], ref[rows, upper]


def forward_kernel(n, qg_ref, kv_ref, front_ref, code_ref, table_ref, stats_ref):
    heads = qg_ref.shape[1] // (2 * HEAD_DIM)
    flat = n * SLOTS
    stats_ref[...] = jnp.zeros(stats_ref.shape, F32)
    for turn in range(ROUNDS):
        for head in range(heads):
            q, g = blocks(qg_ref, turn, head, heads)
            k, v = blocks(kv_ref, turn, head, heads)
            k_front, v_front = blocks(front_ref, turn, head, heads)
            score = dot_nt(k, q) * SCALE
            score_front = dot_nt(k_front, q) * SCALE
            highest = jnp.maximum(
                jnp.max(score, axis=0, keepdims=True), jnp.max(score_front, axis=0, keepdims=True)
            )
            raised = jnp.exp(score - highest)
            raised_front = jnp.exp(score_front - highest)
            total = jnp.sum(raised + raised_front, axis=0, keepdims=True)
            mixed = jnp.sum(
                raised * dot_nt(v, g) + raised_front * dot_nt(v_front, g), axis=0, keepdims=True
            )
            here = slice(turn * SPAN, (turn + 1) * SPAN)
            stats_ref[head : head + 1, here] = highest + jnp.log(total)
            stats_ref[heads + head : heads + head + 1, here] = mixed / total
    chosen = hot(iota((ROUNDS * SPAN, flat), 0) == code_ref[0:1, :])
    by_slot = picked(stats_ref[...], chosen, dot)
    keep = (iota((SLOTS, flat), 1) & 7) == iota((SLOTS, flat), 0)
    groups = [jnp.where(keep, by_slot[i : i + 1], 0.0) for i in range(2 * heads)]
    groups.append(jnp.zeros((LANES - 2 * heads * SLOTS, flat), F32))
    spread = jnp.concatenate(groups, axis=0)
    owner = hot((iota((n, flat), 1) >> 3) == iota((n, flat), 0))
    table_ref[...] = sum(dot_nt(owner, part.astype(BF16)) for part in three_parts(spread))


def home_kernel(n, heads, table_ref, slots_ref, back_ref):
    tokens = slots_ref.shape[1]
    rows = 2 * heads * SLOTS
    values = jnp.transpose(table_ref[...])[:rows]
    row_slot = iota((SLOTS, tokens), 0)
    members = []
    followers = []
    keeps = []
    logs = []
    dots = []
    for turn in range(ROUNDS):
        target, sub = slot_rows(slots_ref, turn)
        member = hot(iota((n, tokens), 0) == target)
        members.append(member)
        followers.append(hot(iota((n, tokens), 0) == ((target + n - 1) & (n - 1))))
        keep = row_slot == sub
        keeps.append(keep)
        here = picked(values, member, dot)
        read = [
            jnp.sum(jnp.where(keep, here[i * SLOTS : (i + 1) * SLOTS], 0.0), axis=0, keepdims=True)
            for i in range(2 * heads)
        ]
        logs.append(read[:heads])
        dots.append(read[heads:])
    shares = [[None] * heads for _ in range(ROUNDS)]
    means = []
    for head in range(heads):
        highest = jnp.maximum(logs[0][head], logs[1][head])
        raised = [jnp.exp(logs[turn][head] - highest) for turn in range(ROUNDS)]
        total = raised[0] + raised[1]
        for turn in range(ROUNDS):
            shares[turn][head] = raised[turn] / total
        means.append(shares[0][head] * dots[0][head] + shares[1][head] * dots[1][head])
    own = []
    behind = []
    one = jnp.ones((1, tokens), F32)
    for turn in range(ROUNDS):
        keep = keeps[turn]
        pieces = [jnp.where(keep, x, 0.0) for x in shares[turn] + means]
        more = [jnp.where(keep, x, 0.0) for x in logs[turn] + [one]]
        used = len(pieces) * SLOTS
        own.append(jnp.concatenate(pieces + [jnp.zeros((LANES - used, tokens), F32)], axis=0))
        both = len(pieces + more) * SLOTS
        behind.append(
            jnp.concatenate(
                [jnp.zeros((used, tokens), F32)]
                + pieces
                + more
                + [jnp.zeros((LANES - used - both, tokens), F32)],
                axis=0,
            )
        )
    result = jnp.zeros((n, LANES), F32)
    for onehot, spread in zip(members + followers, own + behind):
        for part in three_parts(spread):
            result = result + dot_nt(onehot, part.astype(BF16))
    back_ref[...] = result


def backward_kernel(
    n, qg_ref, kv_ref, front_ref, behind_ref, code_ref, stats_ref, back_ref, send_ref, grads_ref
):
    heads = qg_ref.shape[1] // (2 * HEAD_DIM)
    width = heads * HEAD_DIM
    flat = n * SLOTS
    count = 2 * heads
    rows = to_slot_lanes(back_ref[...], count + 3 * heads + 1, n)
    blank = jnp.zeros((8 - count, flat), F32)
    chosen = hot(iota((ROUNDS * SPAN, flat), 0) == code_ref[0:1, :])
    own = picked(jnp.concatenate(rows[:count] + [blank], axis=0), chosen, dot_nt)
    valid = jnp.broadcast_to(rows[-1], (8, flat)) > 0.5
    chosen_behind = hot(iota((ROUNDS * SPAN, flat), 0) == compaction(valid, n))
    blank = jnp.zeros((8 - 3 * heads, flat), F32)
    other = picked(jnp.concatenate(rows[count:-1] + [blank], axis=0), chosen_behind, dot_nt)
    for turn in range(ROUNDS):
        here = slice(turn * SPAN, (turn + 1) * SPAN)
        for head in range(heads):
            q, g = blocks(qg_ref, turn, head, heads)
            k, v = blocks(kv_ref, turn, head, heads)
            k_front, v_front = blocks(front_ref, turn, head, heads)
            q_behind, g_behind = blocks(behind_ref, turn, head, heads)

            def graded(keys, vals, queries, grads, log_total, share, mean):
                weighted = jnp.exp(dot_nt(keys, queries) * SCALE - log_total) * share
                grad_score = weighted * ((dot_nt(vals, grads) - mean) * SCALE)
                return weighted.astype(BF16), grad_score.astype(BF16)

            log_total = stats_ref[head : head + 1, here]
            share = own[head : head + 1, here]
            mean = own[heads + head : heads + head + 1, here]
            weight, scaled = graded(k, v, q, g, log_total, share, mean)
            _, scaled_front = graded(k_front, v_front, q, g, log_total, share, mean)
            weight_behind, scaled_behind = graded(
                k,
                v,
                q_behind,
                g_behind,
                other[2 * heads + head : 2 * heads + head + 1, here],
                other[head : head + 1, here],
                other[heads + head : heads + head + 1, here],
            )
            grad_q = dot_tn(scaled, k) + dot_tn(scaled_front, k_front)
            grad_k = dot(scaled, q) + dot(scaled_behind, q_behind)
            grad_v = dot(weight, g) + dot(weight_behind, g_behind)
            for unit, grad in enumerate((grad_q, grad_k, grad_v)):
                at = unit * width + head * HEAD_DIM
                grads_ref[here, at : at + HEAD_DIM] = grad.astype(BF16)
    send_ref[...] = dot_tn(chosen, grads_ref[...]).astype(BF16)


def final_kernel(slots_ref, ret_ref, dq_ref, dk_ref, dv_ref):
    tokens = slots_ref.shape[1]
    width = dq_ref.shape[1]
    at = iota((ret_ref.shape[0], tokens), 0)
    chosen = hot((at == slots_ref[0:1, :]) | (at == slots_ref[1:2, :]))
    for unit, ref in enumerate((dq_ref, dk_ref, dv_ref)):
        ref[...] = dot_tn(chosen, ret_ref[:, unit * width : (unit + 1) * width]).astype(BF16)


def call(kernel, out, name, scratch=()):
    return pl.pallas_call(
        kernel,
        out_shape=out,
        scratch_shapes=scratch,
        name=name,
        compiler_params=pltpu.CompilerParams(vmem_limit_bytes=48 * 1024 * 1024),
    )


def shape(*dims, dtype=BF16):
    return jax.ShapeDtypeStruct(dims, dtype)


def exchanged(block):
    return lax.all_to_all(block, "seq", split_axis=0, concat_axis=0, tiled=True)


def passed_along(block, distance):
    n = lax.axis_size("seq")
    return lax.ppermute(block, "seq", [((i - distance) % n, i) for i in range(n)])


def body(queries, keys, values, out_grad, sorted_position):
    n = lax.axis_size("seq")
    tokens, width = queries.shape
    heads = width // HEAD_DIM
    flat = n * SLOTS
    places = ROUNDS * SPAN
    placed = lax.all_gather(sorted_position, "head", axis=0, tiled=True)
    send, slots = call(
        functools.partial(pack_kernel, n),
        (shape(flat, 4 * width), shape(8, tokens, dtype=I32)),
        "pack",
    )(placed, queries, out_grad, keys, values)
    arrived = exchanged(send)
    qg, kv, code = call(
        functools.partial(unpack_kernel, n),
        (shape(places, 2 * width), shape(places, 2 * width), shape(8, flat, dtype=I32)),
        "unpack",
    )(arrived)
    front = passed_along(kv, 1)
    behind = passed_along(qg, -1)
    table, stats = call(
        functools.partial(forward_kernel, n),
        (shape(n, LANES, dtype=F32), shape(8, places, dtype=F32)),
        "forward",
    )(qg, kv, front, code)
    back = call(functools.partial(home_kernel, n, heads), shape(n, LANES, dtype=F32), "home")(
        exchanged(table), slots
    )
    grads = call(
        functools.partial(backward_kernel, n),
        shape(flat, 3 * width),
        "backward",
        [pltpu.VMEM((places, 3 * width), BF16)],
    )(qg, kv, front, behind, code, stats, exchanged(back))
    return call(final_kernel, (shape(tokens, width),) * 3, "final")(slots, exchanged(grads))


def solution(mesh):
    in_specs = (
        P("seq", "head"),
        P("seq", "head"),
        P("seq", "head"),
        P("seq", "head"),
        P(None, ("seq", "head")),
    )
    out_specs = (P("seq", "head"), P("seq", "head"), P("seq", "head"))
    return jax.shard_map(body, mesh=mesh, in_specs=in_specs, out_specs=out_specs, check_vma=False)
```

profile of v0, /device:TPU:1, one launch (start us, length us, event | category | flops | bytes accessed | tf_op | source)
XLA Modules:
  0.0 190.2 jit_solution(4023022320702743239)
XLA Ops:
  0.6 8.8 %all-gather = s32[4,2,64]{2,1,0:T(2,128)S(1)} all-gather(s32[1,2,64]{2,1,0:T(2,128)} %bitcast.22), channel_id=1, replica_groups=mesh['seq'=128,'head'=4] {'head'}, dimensions={0}, use_global_device_ids=true | all-gather | bytes 2560 | tf_op jit(solution)/shard_map/all_gather | solution.py:319
  9.4 0.0 copy-start
  9.4 0.9 copy-done
  10.3 0.0 copy-start.1
  10.3 0.9 copy-done.1
  11.2 0.0 copy-start.2
  11.2 0.9 copy-done.2
  12.1 0.0 copy-start.3
  12.1 0.9 copy-done.3
  13.0 1.1 pack.1
  14.2 71.6 %all_to_all.44 = bf16[128,8,1024]{2,1,0:T(8,128)(2,1)S(1)} all-to-all(bf16[128,8,1024]{2,1,0:T(8,128)(2,1)S(1)} %bitcast.17), channel_id=1, replica_groups=mesh['seq'=128,'head'=4] {'seq'}, dimensions={0} | all-to-all | bytes 4194304 | tf_op jit(solution)/shard_map/all_to_all | solution.py:305
  85.7 1.5 unpack.1
  87.2 4.4 %collective-permute-start = (bf16[512,512]{1,0:T(8,128)(2,1)S(1)}, bf16[512,512]{1,0:T(8,128)(2,1)S(1)}, u32[]{:S(2)}, u32[]{:S(2)}) collective-permute-start(bf16[512,512]{1,0:T(8,128)(2,1)S(1)} %get-tuple-element.13.kv_ref), channel_id=1, source_target_pairs={{508,0},{0,4},{4,8},{8,12},{12,16},{16,20},{20,24},{24,28},{28,32}... | collective-permute-start | bytes 1572872 | tf_op jit(solution)/shard_map/ppermute | solution.py:310
  91.7 1.9 %collective-permute-start.1 = (bf16[512,512]{1,0:T(8,128)(2,1)S(1)}, bf16[512,512]{1,0:T(8,128)(2,1)S(1)}, u32[]{:S(2)}, u32[]{:S(2)}) collective-permute-start(bf16[512,512]{1,0:T(8,128)(2,1)S(1)} %get-tuple-element.12.qg_ref), channel_id=1, source_target_pairs={{4,0},{8,4},{12,8},{16,12},{20,16},{24,20},{28,24},{32,28},{36,32}... | collective-permute-start | bytes 1572872 | tf_op jit(solution)/shard_map/ppermute | solution.py:310
  93.6 4.2 %collective-permute-done.front_ref = bf16[512,512]{1,0:T(8,128)(2,1)S(1)} collective-permute-done((bf16[512,512]{1,0:T(8,128)(2,1)S(1)}, bf16[512,512]{1,0:T(8,128)(2,1)S(1)}, u32[]{:S(2)}, u32[]{:S(2)}) %collective-permute-start) | collective-permute-done | bytes 524320 | tf_op jit(solution)/shard_map/ppermute | solution.py:310
  97.8 1.9 %forward.1 = (f32[128,128]{1,0:T(8,128)S(1)}, f32[8,512]{1,0:T(8,128)S(1)}) custom-call(bf16[512,512]{1,0:T(8,128)(2,1)S(1)} %get-tuple-element.12.qg_ref, bf16[512,512]{1,0:T(8,128)(2,1)S(1)} %get-tuple-element.13.kv_ref, bf16[512,512]{1,0:T(8,128)(2,1)S(1)} %collective-permute-done.front_ref, s32[8,1024]{1,0:T(8,128)S(1)} %get-tuple-element.14.code_ref), custom_call_target="tpu_custom_call" | custom-call | tf_op jit(solution)/shard_map/forward/pallas_call | solution.py:333
  99.7 20.3 %all_to_all.45 = f32[128,1,128]{2,1,0:T(1,128)S(1)} all-to-all(f32[128,1,128]{2,1,0:T(1,128)S(1)} %bitcast.20), channel_id=1, replica_groups=mesh['seq'=128,'head'=4] {'seq'}, dimensions={0} | all-to-all | bytes 131072 | tf_op jit(solution)/shard_map/all_to_all | solution.py:305
  120.0 1.3 home.1
  121.2 5.7 %all-to-all-start.2 = ((f32[128,1,128]{2,1,0:T(1,128)}), f32[128,1,128]{2,1,0:T(1,128)S(1)}, u32[]{:S(2)}, u32[]{:S(2)}) async-start(f32[128,1,128]{2,1,0:T(1,128)} %bitcast.8), calls=%async_computation.2 | async-start | bytes 131072 | tf_op jit(solution)/shard_map/all_to_all | solution.py:305
  126.9 0.0 collective-permute-done.1.behind_ref
  127.0 11.5 %all-to-all-done.2 = f32[128,1,128]{2,1,0:T(1,128)S(1)} async-done(((f32[128,1,128]{2,1,0:T(1,128)}), f32[128,1,128]{2,1,0:T(1,128)S(1)}, u32[]{:S(2)}, u32[]{:S(2)}) %all-to-all-start.2) | async-done | bytes 65568 | tf_op jit(solution)/shard_map/all_to_all | solution.py:305
  138.5 4.3 %backward.1 = bf16[1024,768]{1,0:T(8,128)(2,1)S(1)} custom-call(bf16[512,512]{1,0:T(8,128)(2,1)S(1)} %get-tuple-element.12.qg_ref, bf16[512,512]{1,0:T(8,128)(2,1)S(1)} %get-tuple-element.13.kv_ref, bf16[512,512]{1,0:T(8,128)(2,1)S(1)} %collective-permute-done.front_ref, bf16[512,512]{1,0:T(8,128)(2,1)S(1)} %collective-permute-done.1.behind_ref, ...), custom_call_target="tpu_custom_call" | custom-call | tf_op jit(solution)/shard_map/backward/pallas_call | solution.py:341
  142.8 46.1 %all_to_all.46 = bf16[128,8,768]{2,1,0:T(8,128)(2,1)S(1)} all-to-all(bf16[128,8,768]{2,1,0:T(8,128)(2,1)S(1)} %bitcast.16), channel_id=1, replica_groups=mesh['seq'=128,'head'=4] {'seq'}, dimensions={0} | all-to-all | bytes 3145728 | tf_op jit(solution)/shard_map/all_to_all | solution.py:305
  188.9 1.3 final.1
Async XLA Ops:
  9.4 0.9 copy-start
  10.3 0.9 copy-start.1
  11.2 0.9 copy-start.2
  12.1 0.9 copy-start.3
  87.2 10.6 %collective-permute-start = (bf16[512,512]{1,0:T(8,128)(2,1)S(1)}, bf16[512,512]{1,0:T(8,128)(2,1)S(1)}, u32[]{:S(2)}, u32[]{:S(2)}) collective-permute-start(bf16[512,512]{1,0:T(8,128)(2,1)S(1)} %get-tuple-element.13.kv_ref), channel_id=1, source_target_pairs={{508,0},{0,4},{4,8},{8,12},{12,16},{16,20},{20,24},{24,28},{28,32}... | collective-permute-start | bytes 1572872 | tf_op jit(solution)/shard_map/ppermute | solution.py:310
  91.7 35.3 %collective-permute-start.1 = (bf16[512,512]{1,0:T(8,128)(2,1)S(1)}, bf16[512,512]{1,0:T(8,128)(2,1)S(1)}, u32[]{:S(2)}, u32[]{:S(2)}) collective-permute-start(bf16[512,512]{1,0:T(8,128)(2,1)S(1)} %get-tuple-element.12.qg_ref), channel_id=1, source_target_pairs={{4,0},{8,4},{12,8},{16,12},{20,16},{24,20},{28,24},{32,28},{36,32}... | collective-permute-start | bytes 1572872 | tf_op jit(solution)/shard_map/ppermute | solution.py:310
  121.2 17.3 %all-to-all-start.2 = ((f32[128,1,128]{2,1,0:T(1,128)}), f32[128,1,128]{2,1,0:T(1,128)S(1)}, u32[]{:S(2)}, u32[]{:S(2)}) async-start(f32[128,1,128]{2,1,0:T(1,128)} %bitcast.8), calls=%async_computation.2 | async-start | bytes 131072 | tf_op jit(solution)/shard_map/all_to_all | solution.py:305
where the time goes:
time: 191 us; the launch traced here: 190 us
  blocking collectives  147 us (77%)
  waiting for transfers between devices  15.7 us (8%)
  starting transfers between devices  12.1 us (6%)
  Pallas kernels  11.4 us (6%)
  local copies, waits for them, and re-layouts  3.62 us (2%)
    all_to_all x3, blocking collectives, exchanged(): return lax.all_to_all(block, 'seq', split_axis=0, concat_axis=0, tiled=True)  138 us
    all_to_all x1, waiting for transfers between devices, exchanged(): return lax.all_to_all(block, 'seq', split_axis=0, concat_axis=0, tiled=True)  11.5 us
    all_gather x1, blocking collectives, body(): placed = lax.all_gather(sorted_position, 'head', axis=0, tiled=True)  8.78 us
    ppermute x2, starting transfers between devices, passed_along(): lax.ppermute(block, 'seq', [((i - distance) % n, i) for i in range(n)])  6.36 us
    all_to_all x1, starting transfers between devices, exchanged(): return lax.all_to_all(block, 'seq', split_axis=0, concat_axis=0, tiled=True)  5.7 us
    pallas_call x1, Pallas kernels, body(): call(functools.partial(backward_kernel, n), shape(flat, 3 * width), 'back...  4.26 us
    ppermute x2, waiting for transfers between devices, passed_along(): lax.ppermute(block, 'seq', [((i - distance) % n, i) for i in range(n)])  4.18 us
  transfers between devices with their start and end apart: 3, of which 2 were waited for; matrix products, arithmetic and copies ran while one was open for 0% of the time, Pallas kernels for 2%

commit v1 on v0

v1 whole, which is shorter than its diff:
```python
import functools
import math

import jax
import jax.numpy as jnp
from jax import lax
from jax.experimental import pallas as pl
from jax.experimental.pallas import tpu as pltpu
from jax.sharding import PartitionSpec as P

HEAD_DIM = 128
SPAN = 256
ROUNDS = 2
CAP = 4
GROUP = 4
SLOTS = 8
HALVES = 2
LANES = 128
EMPTY = 8.0
SCALE = 1.0 / math.sqrt(HEAD_DIM)
F32 = jnp.float32
BF16 = jnp.bfloat16
I32 = jnp.int32


def iota(shape, dim):
    return lax.broadcasted_iota(I32, shape, dim)


def hot(condition):
    return jnp.where(condition, 1.0, 0.0).astype(BF16)


def dot(a, b):
    return lax.dot_general(a, b, (((1,), (0,)), ((), ())), preferred_element_type=F32)


def dot_nt(a, b):
    return lax.dot_general(a, b, (((1,), (1,)), ((), ())), preferred_element_type=F32)


def dot_tn(a, b):
    return lax.dot_general(a, b, (((0,), (0,)), ((), ())), preferred_element_type=F32)


def three_parts(x):
    high = x.astype(BF16).astype(F32)
    rest = x - high
    middle = rest.astype(BF16).astype(F32)
    return high, middle, (rest - middle).astype(BF16).astype(F32)


def picked(x, onehot, product):
    rows = x.shape[0]
    stacked = jnp.concatenate(three_parts(x), axis=0).astype(BF16)
    out = product(stacked, onehot)
    return out[:rows] + out[rows : 2 * rows] + out[2 * rows :]


def hot_rows(code):
    at = iota((SPAN, LANES), 0).astype(F32).astype(BF16)
    code = code.astype(F32).astype(BF16)
    pieces = [
        jnp.where(at == code[:, i : i + LANES], jnp.ones_like(at), jnp.zeros_like(at))
        for i in range(0, code.shape[1], LANES)
    ]
    return jnp.concatenate(pieces, axis=1)


def ranked(mine):
    before = hot(iota((LANES, LANES), 0) < iota((LANES, LANES), 1))
    chunks = mine.shape[1] // LANES
    stacked = jnp.concatenate([mine[:, i * LANES : (i + 1) * LANES] for i in range(chunks)], axis=0)
    rank = dot(stacked.astype(BF16), before)
    totals = jnp.sum(stacked, axis=1, keepdims=True)
    running = jnp.zeros((8, 1), F32)
    pieces = []
    for i in range(chunks):
        here = slice(i * 8, (i + 1) * 8)
        pieces.append(jnp.where(stacked[here] > 0.0, rank[here] + running, -1.0))
        running = running + totals[here]
    return jnp.concatenate(pieces, axis=1).astype(I32)


def to_slot_lanes(table, groups, n):
    rows = groups * SLOTS
    flat = n * SLOTS
    owner = hot((iota((n, flat), 1) >> 3) == iota((n, flat), 0))
    spread = picked(jnp.transpose(table)[:rows], owner, dot)
    keep = (iota((SLOTS, flat), 1) & 7) == iota((SLOTS, flat), 0)
    return [
        jnp.sum(jnp.where(keep, spread[g * SLOTS : (g + 1) * SLOTS], 0.0), axis=0, keepdims=True)
        for g in range(groups)
    ]


def pack_kernel(n, pos_ref, held_ref, send_ref, slots_ref):
    tokens = held_ref.shape[0]
    width = held_ref.shape[1] // 4
    quarters = pos_ref.shape[0] // ROUNDS
    groups = n // GROUP
    tall = groups * SLOTS
    before = hot(iota((tokens, tokens), 0) < iota((tokens, tokens), 1))
    main = [[], []]
    edge = []
    slots = []
    for turn in range(ROUNDS):
        places = jnp.concatenate(
            [pos_ref[x * ROUNDS + turn : x * ROUNDS + turn + 1, :] for x in range(quarters)], axis=1
        )
        span = places >> 8
        member = iota((n, tokens), 0) == span
        earlier = dot(hot(member), before)
        rank = jnp.sum(jnp.where(member, earlier, 0.0), axis=0, keepdims=True).astype(I32)
        slots.append(span * CAP + rank)
        row = (span >> 2) * SLOTS + (span & 1) * CAP + rank
        for half in range(HALVES):
            main[half].append(hot_rows(jnp.where(((span >> 1) & 1) == half, row, -1)))
        last = (span & 3) == 3
        row = (((span + 1) & (n - 1)) >> 2) * SLOTS + rank
        edge.append(
            hot_rows(jnp.where(last, row, -1)) + hot_rows(jnp.where(last, row + CAP, -1))
        )
    slots_ref[...] = jnp.concatenate(slots + [jnp.zeros((8 - ROUNDS, tokens), I32)], axis=0)
    chosen = jnp.concatenate(main[0] + main[1] + edge, axis=0)
    filled = dot(chosen, jnp.ones((tokens, LANES), BF16))
    mark = jnp.where(iota(filled.shape, 1) == 0, EMPTY * (1.0 - filled), 0.0)
    mark = jnp.concatenate([mark] * (width // LANES), axis=1)

    def store(column, part):
        tiles = [
            part[turn * tall : (turn + 1) * tall, head * HEAD_DIM : (head + 1) * HEAD_DIM].reshape(
                groups, 1, SLOTS, HEAD_DIM
            )
            for turn in range(ROUNDS)
            for head in range(part.shape[1] // HEAD_DIM)
        ]
        rows = jnp.concatenate(tiles, axis=1).reshape(n * SLOTS, HEAD_DIM)
        send_ref[:, column * HEAD_DIM : (column + 1) * HEAD_DIM] = rows.astype(BF16)

    both = ROUNDS * tall
    edges = []
    for unit in range(4):
        rows = chosen if unit >= 2 else chosen[: HALVES * both]
        part = dot(rows, held_ref[:, unit * width : (unit + 1) * width])
        for half in range(HALVES):
            rows = slice(half * both, (half + 1) * both)
            store(half * 4 + unit, part[rows] + mark[rows] if unit == 0 else part[rows])
        edges.append(part[HALVES * both :])
    upper = (iota(edges[2].shape, 0) & CAP) == 0
    store(HALVES * 4, jnp.where(upper, edges[2], edges[3]) + mark[HALVES * both :])


def unpack_kernel(n, recv_ref, rows_ref, front_ref, head_ref, code_ref, chosen_ref):
    flat = n * SLOTS
    wide = 4 * HEAD_DIM
    lead = hot(iota((8, LANES), 1) == 0)
    row = iota((8, flat), 0)
    mine = jnp.zeros((8, flat), F32)
    for block in range(HALVES + 1):
        first = dot_nt(lead, recv_ref[:, block * wide : block * wide + LANES])
        mine = jnp.where(((row >> 1) == block) & (first < EMPTY - 1.0), 1.0, mine)
    mine = jnp.where(((iota((8, flat), 1) >> 2) & 1) == (row & 1), mine, 0.0)
    code = ranked(mine)
    code_ref[...] = code
    for half in range(HALVES):
        here = slice(half * 2 * SPAN, (half + 1) * 2 * SPAN)
        chosen = jnp.concatenate(
            [hot_rows(code[half * 2 + span : half * 2 + span + 1]) for span in range(2)], axis=0
        )
        chosen_ref[here, :] = chosen
        rows = dot(chosen, recv_ref[:, half * wide : (half + 1) * wide]).astype(BF16)
        rows_ref[here, :] = rows
        if half == 0:
            head_ref[...] = rows[:SPAN, : 2 * HEAD_DIM]
    for kind in range(2):
        chosen = hot_rows(code[2 * HALVES + kind : 2 * HALVES + kind + 1])
        front_ref[kind * SPAN : (kind + 1) * SPAN, :] = dot(
            chosen, recv_ref[:, HALVES * wide : HALVES * wide + LANES]
        ).astype(BF16)


def unit_of(ref, span, unit):
    return ref[span * SPAN : (span + 1) * SPAN, unit * HEAD_DIM : (unit + 1) * HEAD_DIM]


def forward_kernel(n, rows_ref, front_ref, chosen_ref, table_ref, stats_ref):
    flat = n * SLOTS
    stats_ref[...] = jnp.zeros(stats_ref.shape, F32)
    for span in range(GROUP):
        q, g, k, v = (unit_of(rows_ref, span, unit) for unit in range(4))
        if span == 0:
            k_front, v_front = unit_of(front_ref, 0, 0), unit_of(front_ref, 1, 0)
        else:
            k_front, v_front = unit_of(rows_ref, span - 1, 2), unit_of(rows_ref, span - 1, 3)
        score = dot_nt(k, q) * SCALE
        score_front = dot_nt(k_front, q) * SCALE
        highest = jnp.maximum(
            jnp.max(score, axis=0, keepdims=True), jnp.max(score_front, axis=0, keepdims=True)
        )
        raised = jnp.exp(score - highest)
        raised_front = jnp.exp(score_front - highest)
        total = jnp.sum(raised + raised_front, axis=0, keepdims=True)
        mixed = jnp.sum(
            raised * dot_nt(v, g) + raised_front * dot_nt(v_front, g), axis=0, keepdims=True
        )
        here = slice(span * SPAN, (span + 1) * SPAN)
        stats_ref[0:1, here] = highest + jnp.log(total)
        stats_ref[1:2, here] = mixed / total
    keep = (iota((SLOTS, flat), 1) & 7) == iota((SLOTS, flat), 0)
    by_half = []
    for half in range(HALVES):
        here = slice(half * 2 * SPAN, (half + 1) * 2 * SPAN)
        by_half.append(picked(stats_ref[:, here], chosen_ref[here, :], dot))
    spread = [
        jnp.where(keep, by_half[half][kind : kind + 1], 0.0)
        for kind in range(2)
        for half in range(HALVES)
    ]
    spread.append(jnp.zeros((LANES - len(spread) * SLOTS, flat), F32))
    spread = jnp.concatenate(spread, axis=0)
    owner = hot((iota((n, flat), 1) >> 3) == iota((n, flat), 0))
    table_ref[...] = sum(dot_nt(owner, part.astype(BF16)) for part in three_parts(spread))


def home_kernel(n, heads, table_ref, slots_ref, back_ref):
    tokens = slots_ref.shape[1]
    wide = GROUP * CAP
    values = jnp.transpose(table_ref[...])[: 2 * wide]
    device = iota((n, tokens), 0)
    lane = iota((wide, tokens), 0)
    span_slot = []
    logs = []
    dots = []
    for turn in range(ROUNDS):
        slot = slots_ref[turn : turn + 1, :]
        group = slot >> 4
        keep = lane == (slot & 15)
        span_slot.append((group, keep, slot))
        for head in range(heads):
            member = hot(device == group * GROUP + turn * heads + head)
            here = picked(values, member, dot)
            logs.append(jnp.sum(jnp.where(keep, here[:wide], 0.0), axis=0, keepdims=True))
            dots.append(jnp.sum(jnp.where(keep, here[wide:], 0.0), axis=0, keepdims=True))
    members = []
    values = []
    one = jnp.ones((1, tokens), F32)
    for head in range(heads):
        log_0, log_1 = logs[head], logs[heads + head]
        highest = jnp.maximum(log_0, log_1)
        raised = [jnp.exp(log_0 - highest), jnp.exp(log_1 - highest)]
        total = raised[0] + raised[1]
        shares = [raised[0] / total, raised[1] / total]
        mean = shares[0] * dots[head] + shares[1] * dots[heads + head]
        for turn in range(ROUNDS):
            group, keep, slot = span_slot[turn]
            mine = turn * heads + head
            members.append(hot(device == group * GROUP + mine))
            values.append(
                jnp.concatenate(
                    [jnp.where(keep, x, 0.0) for x in (shares[turn], mean)]
                    + [jnp.zeros((LANES - 2 * wide, tokens), F32)],
                    axis=0,
                )
            )
            ahead = ((group + n // GROUP - 1) & (n // GROUP - 1)) * GROUP + mine
            members.append(hot(device == ahead))
            edge = iota((SLOTS, tokens), 0) == jnp.where((slot & 12) == 0, slot & 3, -1)
            values.append(
                jnp.concatenate(
                    [jnp.zeros((2 * wide, tokens), F32)]
                    + [jnp.where(edge, x, 0.0) for x in (shares[turn], mean, logs[mine], one)]
                    + [jnp.zeros((LANES - 2 * wide - 4 * SLOTS, tokens), F32)],
                    axis=0,
                )
            )
    left = jnp.concatenate(members, axis=1)
    right = jnp.concatenate(values, axis=1)
    back_ref[...] = sum(dot_nt(left, part.astype(BF16)) for part in three_parts(right))


def backward_kernel(
    n,
    rows_ref,
    front_ref,
    behind_ref,
    chosen_ref,
    code_ref,
    stats_ref,
    back_ref,
    send_ref,
    grads_ref,
):
    flat = n * SLOTS
    lanes = to_slot_lanes(back_ref[...], 2 * HALVES + 4, n)
    shares = []
    means = []
    for half in range(HALVES):
        chosen = chosen_ref[half * 2 * SPAN : (half + 1) * 2 * SPAN, :]
        pair = jnp.concatenate(
            [lanes[half], lanes[HALVES + half], jnp.zeros((6, flat), F32)], axis=0
        )
        own = picked(pair, chosen, dot_nt)
        for span in range(2):
            shares.append(own[0:1, span * SPAN : (span + 1) * SPAN])
            means.append(own[1:2, span * SPAN : (span + 1) * SPAN])
    edge = lanes[2 * HALVES :]
    chosen = hot_rows(ranked(jnp.broadcast_to(edge[3], (8, flat)))[0:1])
    other = picked(
        jnp.concatenate(edge[:3] + [jnp.zeros((5, flat), F32)], axis=0), chosen, dot_nt
    )

    def graded(keys, vals, queries, grads, log_total, share, mean):
        weighted = jnp.exp(dot_nt(keys, queries) * SCALE - log_total) * share
        grad_score = weighted * ((dot_nt(vals, grads) - mean) * SCALE)
        return weighted.astype(BF16), grad_score.astype(BF16)

    def put(span, unit, grad):
        grads_ref[span * SPAN : (span + 1) * SPAN, unit * HEAD_DIM : (unit + 1) * HEAD_DIM] = (
            grad.astype(BF16)
        )

    grad_k = None
    grad_v = None
    for span in range(GROUP):
        q, g, k, v = (unit_of(rows_ref, span, unit) for unit in range(4))
        log_total = stats_ref[0:1, span * SPAN : (span + 1) * SPAN]
        if span == 0:
            k_front, v_front = unit_of(front_ref, 0, 0), unit_of(front_ref, 1, 0)
        else:
            k_front, v_front = unit_of(rows_ref, span - 1, 2), unit_of(rows_ref, span - 1, 3)
        row = (log_total, shares[span], means[span])
        weight, scaled = graded(k, v, q, g, *row)
        weight_front, scaled_front = graded(k_front, v_front, q, g, *row)
        put(span, 0, dot_tn(scaled, k) + dot_tn(scaled_front, k_front))
        if span > 0:
            put(span - 1, 1, grad_k + dot(scaled_front, q))
            put(span - 1, 2, grad_v + dot(weight_front, g))
        grad_k = dot(scaled, q)
        grad_v = dot(weight, g)
    q, g = behind_ref[:, :HEAD_DIM], behind_ref[:, HEAD_DIM:]
    weight, scaled = graded(k, v, q, g, other[2:3], other[0:1], other[1:2])
    put(GROUP - 1, 1, grad_k + dot(scaled, q))
    put(GROUP - 1, 2, grad_v + dot(weight, g))
    wide = 3 * HEAD_DIM
    codes = jnp.transpose(code_ref[...].astype(F32)).astype(I32)
    for half in range(HALVES):
        across = jnp.concatenate(
            [hot(iota((flat, SPAN), 1) == codes[:, i : i + 1]) for i in (half * 2, half * 2 + 1)],
            axis=1,
        )
        send_ref[:, half * wide : (half + 1) * wide] = dot(
            across, grads_ref[half * 2 * SPAN : (half + 1) * 2 * SPAN, :]
        ).astype(BF16)


def final_kernel(n, slots_ref, ret_ref, dq_ref, dk_ref, dv_ref):
    heads = dq_ref.shape[1] // HEAD_DIM
    flat = n * SLOTS
    wide = 3 * HEAD_DIM
    slots = jnp.transpose(slots_ref[...].astype(F32)).astype(I32)
    at = iota((slots.shape[0], flat), 1)
    for head in range(heads):
        total = None
        for half in range(HALVES):
            match = []
            for turn in range(ROUNDS):
                slot = slots[:, turn : turn + 1]
                row = ((slot >> 4) * GROUP + turn * heads + head) * SLOTS + (slot & 7)
                match.append(at == jnp.where(((slot >> 3) & 1) == half, row, -1))
            part = dot(hot(match[0] | match[1]), ret_ref[:, half * wide : (half + 1) * wide])
            total = part if total is None else total + part
        for unit, ref in enumerate((dq_ref, dk_ref, dv_ref)):
            ref[:, head * HEAD_DIM : (head + 1) * HEAD_DIM] = total[
                :, unit * HEAD_DIM : (unit + 1) * HEAD_DIM
            ].astype(BF16)


def call(kernel, out, name, scratch=()):
    return pl.pallas_call(
        kernel,
        out_shape=out,
        scratch_shapes=scratch,
        name=name,
        compiler_params=pltpu.CompilerParams(vmem_limit_bytes=24 * 1024 * 1024),
    )


def shape(*dims, dtype=BF16):
    return jax.ShapeDtypeStruct(dims, dtype)


def exchanged(block):
    return lax.all_to_all(block, "seq", split_axis=0, concat_axis=0, tiled=True)


def passed_along(block, distance):
    n = lax.axis_size("seq")
    return lax.ppermute(block, "seq", [((i - distance) % n, i) for i in range(n)])


def body(queries, keys, values, out_grad, sorted_position):
    n = lax.axis_size("seq")
    tokens, width = queries.shape
    heads = width // HEAD_DIM
    flat = n * SLOTS
    places = GROUP * SPAN
    placed = lax.all_gather(sorted_position, "head", axis=0, tiled=True)
    send, slots = call(
        functools.partial(pack_kernel, n),
        (shape(flat, (4 * HALVES + 1) * HEAD_DIM), shape(8, tokens, dtype=I32)),
        "pack",
    )(placed, jnp.concatenate([queries, out_grad, keys, values], axis=1))
    rows, front, first, code, chosen = call(
        functools.partial(unpack_kernel, n),
        (
            shape(places, 4 * HEAD_DIM),
            shape(2 * SPAN, HEAD_DIM),
            shape(SPAN, 2 * HEAD_DIM),
            shape(8, flat, dtype=I32),
            shape(places, flat),
        ),
        "unpack",
    )(exchanged(send))
    behind = passed_along(first, -GROUP)
    table, stats = call(
        functools.partial(forward_kernel, n),
        (shape(n, LANES, dtype=F32), shape(8, places, dtype=F32)),
        "forward",
    )(rows, front, chosen)
    back = call(functools.partial(home_kernel, n, heads), shape(n, LANES, dtype=F32), "home")(
        exchanged(table), slots
    )
    grads = call(
        functools.partial(backward_kernel, n),
        shape(flat, 3 * HALVES * HEAD_DIM),
        "backward",
        [pltpu.VMEM((places, 3 * HEAD_DIM), BF16)],
    )(rows, front, behind, chosen, code, stats, exchanged(back))
    return call(functools.partial(final_kernel, n), (shape(tokens, width),) * 3, "final")(
        slots, exchanged(grads)
    )


def solution(mesh):
    in_specs = (
        P("seq", "head"),
        P("seq", "head"),
        P("seq", "head"),
        P("seq", "head"),
        P(None, ("seq", "head")),
    )
    out_specs = (P("seq", "head"), P("seq", "head"), P("seq", "head"))
    return jax.shard_map(body, mesh=mesh, in_specs=in_specs, out_specs=out_specs, check_vma=False)
```

time: 191 us -> 186 us (0.974)
  blocking collectives: 147 us -> 132 us
  starting transfers between devices: 12.1 us -> 22.2 us
  local copies, waits for them, and re-layouts: 3.62 us -> 0.65 us
  Pallas kernels: 11.4 us -> 14.1 us
    all_to_all x3 -> x2, blocking collectives: 138 us -> 123 us  [exchanged(): return lax.all_to_all(block, 'seq', split_axis=0, concat_axis=0, tiled=True)]
    all_to_all x1 -> x2, starting transfers between devices: 5.7 us -> 13.9 us  [exchanged(): return lax.all_to_all(block, 'seq', split_axis=0, concat_axis=0, tiled=True)]
    ppermute x2 -> x1, waiting for transfers between devices: 4.18 us -> 0.01 us  [passed_along(): lax.ppermute(block, 'seq', [((i - distance) % n, i) for i in range(n)])]
    all_to_all x1 -> x2, waiting for transfers between devices: 11.5 us -> 14.6 us  [exchanged(): return lax.all_to_all(block, 'seq', split_axis=0, concat_axis=0, tiled=True)]
    unnamed x8 -> x2, local copies, waits for them, and re-layouts: 3.62 us -> 0.65 us
    ppermute x2 -> x1, starting transfers between devices: 6.36 us -> 8.24 us  [passed_along(): lax.ppermute(block, 'seq', [((i - distance) % n, i) for i in range(n)])]
  transfers between devices with their start and end apart: 3 -> 3, of which waited for: 2 -> 2; matrix products, arithmetic and copies ran while one was open for 0% -> 0% of each run, Pallas kernels for 2% -> 1%
where the time goes in v1:
time: 186 us; the launch traced here: 185 us
  blocking collectives  132 us (71%)
  starting transfers between devices  22.2 us (12%)
  waiting for transfers between devices  14.6 us (8%)
  Pallas kernels  14.1 us (8%)
    all_to_all x2, blocking collectives, exchanged(): return lax.all_to_all(block, 'seq', split_axis=0, concat_axis=0, tiled=True)  123 us
    all_to_all x2, waiting for transfers between devices, exchanged(): return lax.all_to_all(block, 'seq', split_axis=0, concat_axis=0, tiled=True)  14.6 us
    all_to_all x2, starting transfers between devices, exchanged(): return lax.all_to_all(block, 'seq', split_axis=0, concat_axis=0, tiled=True)  13.9 us
    all_gather x1, blocking collectives, body(): placed = lax.all_gather(sorted_position, 'head', axis=0, tiled=True)  8.78 us
    ppermute x1, starting transfers between devices, passed_along(): lax.ppermute(block, 'seq', [((i - distance) % n, i) for i in range(n)])  8.24 us
    pallas_call x1, Pallas kernels, body(): call(functools.partial(backward_kernel, n), shape(flat, 3 * HALVES * HEAD...  4.5 us
  transfers between devices with their start and end apart: 3, of which 2 were waited for; matrix products, arithmetic and copies ran while one was open for 0% of the time, Pallas kernels for 1%

profile of v1, /device:TPU:1, one launch (start us, length us, event | category | flops | bytes accessed | tf_op | source)
XLA Modules:
  0.0 185.2 jit_solution(16364174611808131529)
XLA Ops:
  0.6 8.8 %all-gather = s32[4,2,64]{2,1,0:T(2,128)S(1)} all-gather(s32[1,2,64]{2,1,0:T(2,128)} %bitcast.21), channel_id=1, replica_groups=mesh['seq'=128,'head'=4] {'head'}, dimensions={0}, use_global_device_ids=true | all-gather | bytes 2560 | tf_op jit(solution)/shard_map/all_gather | solution.py:408
  9.4 1.2 pad_maximum_fusion.held_ref
  10.6 1.3 pack.1
  11.9 76.9 %all_to_all.44 = bf16[128,8,1152]{2,1,0:T(8,128)(2,1)S(1)} all-to-all(bf16[128,8,1152]{2,1,0:T(8,128)(2,1)S(1)} %bitcast.17), channel_id=1, replica_groups=mesh['seq'=128,'head'=4] {'seq'}, dimensions={0} | all-to-all | bytes 4718592 | tf_op jit(solution)/shard_map/all_to_all | solution.py:394
  88.8 2.1 %unpack.1 = (bf16[1024,512]{1,0:T(8,128)(2,1)S(1)}, bf16[512,128]{1,0:T(8,128)(2,1)S(1)}, bf16[256,256]{1,0:T(8,128)(2,1)S(1)}, s32[8,1024]{1,0:T(8,128)S(1)}, bf16[1024,1024]{1,0:T(8,128)(2,1)S(1)}) custom-call(bf16[1024,1152]{1,0:T(8,128)(2,1)S(1)} %bitcast.14), custom_call_target="tpu_custom_call" | custom-call | tf_op jit(solution)/shard_map/unpack/pallas_call | solution.py:414
  90.8 0.0 copy-start
  90.9 0.6 copy-done
  91.5 2.6 %forward.1 = (f32[128,128]{1,0:T(8,128)}, f32[8,1024]{1,0:T(8,128)S(1)}) custom-call(bf16[1024,512]{1,0:T(8,128)(2,1)S(1)} %get-tuple-element.14.rows_ref, bf16[512,128]{1,0:T(8,128)(2,1)S(1)} %get-tuple-element.15.front_ref, bf16[1024,1024]{1,0:T(8,128)(2,1)S(1)} %get-tuple-element.17.chosen_ref), custom_call_target="tpu_custom_call" | custom-call | tf_op jit(solution)/shard_map/forward/pallas_call | solution.py:426
  94.1 8.1 %all-to-all-start.1 = ((f32[128,1,128]{2,1,0:T(1,128)}), f32[128,1,128]{2,1,0:T(1,128)S(1)}, u32[]{:S(2)}, u32[]{:S(2)}) async-start(f32[128,1,128]{2,1,0:T(1,128)} %bitcast.5), calls=%async_computation.1 | async-start | bytes 131072 | tf_op jit(solution)/shard_map/all_to_all | solution.py:394
  102.2 8.2 %collective-permute-start = (bf16[256,256]{1,0:T(8,128)(2,1)}, bf16[256,256]{1,0:T(8,128)(2,1)S(1)}, u32[]{:S(2)}, u32[]{:S(2)}) collective-permute-start(bf16[256,256]{1,0:T(8,128)(2,1)} %copy-done), channel_id=1, source_target_pairs={{16,0},{20,4},{24,8},{28,12},{32,16},{36,20},{40,24},{44,28},{48,3... | collective-permute-start | bytes 393224 | tf_op jit(solution)/shard_map/ppermute | solution.py:399
  110.4 3.2 %all-to-all-done.1 = f32[128,1,128]{2,1,0:T(1,128)S(1)} async-done(((f32[128,1,128]{2,1,0:T(1,128)}), f32[128,1,128]{2,1,0:T(1,128)S(1)}, u32[]{:S(2)}, u32[]{:S(2)}) %all-to-all-start.1) | async-done | bytes 65568 | tf_op jit(solution)/shard_map/all_to_all | solution.py:394
  113.6 1.5 home.1
  115.1 5.8 %all-to-all-start.2 = ((f32[128,1,128]{2,1,0:T(1,128)}), f32[128,1,128]{2,1,0:T(1,128)S(1)}, u32[]{:S(2)}, u32[]{:S(2)}) async-start(f32[128,1,128]{2,1,0:T(1,128)} %bitcast.8), calls=%async_computation.2 | async-start | bytes 131072 | tf_op jit(solution)/shard_map/all_to_all | solution.py:394
  120.9 0.0 collective-permute-done.behind_ref
  121.0 11.4 %all-to-all-done.2 = f32[128,1,128]{2,1,0:T(1,128)S(1)} async-done(((f32[128,1,128]{2,1,0:T(1,128)}), f32[128,1,128]{2,1,0:T(1,128)S(1)}, u32[]{:S(2)}, u32[]{:S(2)}) %all-to-all-start.2) | async-done | bytes 65568 | tf_op jit(solution)/shard_map/all_to_all | solution.py:394
  132.4 4.5 %backward.1 = bf16[1024,768]{1,0:T(8,128)(2,1)S(1)} custom-call(bf16[1024,512]{1,0:T(8,128)(2,1)S(1)} %get-tuple-element.14.rows_ref, bf16[512,128]{1,0:T(8,128)(2,1)S(1)} %get-tuple-element.15.front_ref, bf16[256,256]{1,0:T(8,128)(2,1)S(1)} %collective-permute-done.behind_ref, bf16[1024,1024]{1,0:T(8,128)(2,1)S(1)} %get-tuple-element.17.chosen_ref, ...), custom_call_target="tpu_custom_call" | custom-call | tf_op jit(solution)/shard_map/backward/pallas_call | solution.py:434
  136.9 46.2 %all_to_all.45 = bf16[128,8,768]{2,1,0:T(8,128)(2,1)S(1)} all-to-all(bf16[128,8,768]{2,1,0:T(8,128)(2,1)S(1)} %bitcast.16), channel_id=1, replica_groups=mesh['seq'=128,'head'=4] {'seq'}, dimensions={0} | all-to-all | bytes 3145728 | tf_op jit(solution)/shard_map/all_to_all | solution.py:394
  183.0 2.2 %final.1 = (bf16[256,256]{1,0:T(8,128)(2,1)}, bf16[256,256]{1,0:T(8,128)(2,1)}, bf16[256,256]{1,0:T(8,128)(2,1)}) custom-call(s32[8,256]{1,0:T(8,128)S(1)} %get-tuple-element.12.slots_ref, bf16[1024,768]{1,0:T(8,128)(2,1)S(1)} %bitcast.15), custom_call_target="tpu_custom_call" | custom-call | tf_op jit(solution)/shard_map/final/pallas_call | solution.py:440
Async XLA Ops:
  90.8 0.7 copy-start
  94.1 19.6 %all-to-all-start.1 = ((f32[128,1,128]{2,1,0:T(1,128)}), f32[128,1,128]{2,1,0:T(1,128)S(1)}, u32[]{:S(2)}, u32[]{:S(2)}) async-start(f32[128,1,128]{2,1,0:T(1,128)} %bitcast.5), calls=%async_computation.1 | async-start | bytes 131072 | tf_op jit(solution)/shard_map/all_to_all | solution.py:394
  102.2 18.8 %collective-permute-start = (bf16[256,256]{1,0:T(8,128)(2,1)}, bf16[256,256]{1,0:T(8,128)(2,1)S(1)}, u32[]{:S(2)}, u32[]{:S(2)}) collective-permute-start(bf16[256,256]{1,0:T(8,128)(2,1)} %copy-done), channel_id=1, source_target_pairs={{16,0},{20,4},{24,8},{28,12},{32,16},{36,20},{40,24},{44,28},{48,3... | collective-permute-start | bytes 393224 | tf_op jit(solution)/shard_map/ppermute | solution.py:399
  115.1 17.3 %all-to-all-start.2 = ((f32[128,1,128]{2,1,0:T(1,128)}), f32[128,1,128]{2,1,0:T(1,128)S(1)}, u32[]{:S(2)}, u32[]{:S(2)}) async-start(f32[128,1,128]{2,1,0:T(1,128)} %bitcast.8), calls=%async_computation.2 | async-start | bytes 131072 | tf_op jit(solution)/shard_map/all_to_all | solution.py:394

commit v2 on v1

v2 whole, which is shorter than its diff:
```python
import functools
import math

import jax
import jax.numpy as jnp
from jax import lax
from jax.experimental import pallas as pl
from jax.experimental.pallas import tpu as pltpu
from jax.sharding import PartitionSpec as P

HEAD_DIM = 128
SPAN = 256
ROUNDS = 2
CAP = 4
GROUP = 4
SLOTS = 8
HALVES = 2
LANES = 128
EMPTY = 8.0
SCALE = 1.0 / math.sqrt(HEAD_DIM)
F32 = jnp.float32
BF16 = jnp.bfloat16
I32 = jnp.int32


def iota(shape, dim):
    return lax.broadcasted_iota(I32, shape, dim)


def hot(condition):
    return jnp.where(condition, 1.0, 0.0).astype(BF16)


def dot(a, b):
    return lax.dot_general(a, b, (((1,), (0,)), ((), ())), preferred_element_type=F32)


def dot_nt(a, b):
    return lax.dot_general(a, b, (((1,), (1,)), ((), ())), preferred_element_type=F32)


def dot_tn(a, b):
    return lax.dot_general(a, b, (((0,), (0,)), ((), ())), preferred_element_type=F32)


def three_parts(x):
    high = x.astype(BF16).astype(F32)
    rest = x - high
    middle = rest.astype(BF16).astype(F32)
    return high, middle, (rest - middle).astype(BF16).astype(F32)


def picked(x, onehot, product):
    rows = x.shape[0]
    stacked = jnp.concatenate(three_parts(x), axis=0).astype(BF16)
    out = product(stacked, onehot)
    return out[:rows] + out[rows : 2 * rows] + out[2 * rows :]


def hot_rows(code, rows=SPAN):
    at = iota((rows, LANES), 0).astype(F32).astype(BF16)
    code = code.astype(F32).astype(BF16)
    pieces = [
        jnp.where(at == code[:, i : i + LANES], jnp.ones_like(at), jnp.zeros_like(at))
        for i in range(0, code.shape[1], LANES)
    ]
    return jnp.concatenate(pieces, axis=1)


def ranked(mine):
    before = hot(iota((LANES, LANES), 0) < iota((LANES, LANES), 1))
    chunks = mine.shape[1] // LANES
    stacked = jnp.concatenate([mine[:, i * LANES : (i + 1) * LANES] for i in range(chunks)], axis=0)
    rank = dot(stacked.astype(BF16), before)
    totals = jnp.sum(stacked, axis=1, keepdims=True)
    running = jnp.zeros((8, 1), F32)
    pieces = []
    for i in range(chunks):
        here = slice(i * 8, (i + 1) * 8)
        pieces.append(jnp.where(stacked[here] > 0.0, rank[here] + running, -1.0))
        running = running + totals[here]
    return jnp.concatenate(pieces, axis=1).astype(I32)


def pack_kernel(n, pos_ref, held_ref, send_ref, slots_ref):
    tokens = held_ref.shape[0]
    width = held_ref.shape[1] // 4
    heads = width // HEAD_DIM
    quarters = pos_ref.shape[0] // ROUNDS
    tall = n // GROUP * SLOTS
    before = hot(iota((tokens, tokens), 0) < iota((tokens, tokens), 1))
    main = [[], []]
    edge = []
    slots = []
    for turn in range(ROUNDS):
        places = jnp.concatenate(
            [pos_ref[x * ROUNDS + turn : x * ROUNDS + turn + 1, :] for x in range(quarters)], axis=1
        )
        span = places >> 8
        member = hot_rows(span, n)
        earlier = dot(member, before)
        rank = jnp.sum(member.astype(F32) * earlier, axis=0, keepdims=True).astype(I32)
        slots.append(span * CAP + rank)
        row = (span >> 2) * SLOTS + (span & 1) * CAP + rank
        for half in range(HALVES):
            main[half].append(hot_rows(jnp.where(((span >> 1) & 1) == half, row, -1)))
        last = (span & 3) == 3
        row = (((span + 1) & (n - 1)) >> 2) * SLOTS + rank
        edge.append(
            hot_rows(jnp.where(last, row, -1)) + hot_rows(jnp.where(last, row + CAP, -1))
        )
    slots_ref[...] = jnp.concatenate(slots + [jnp.zeros((8 - ROUNDS, tokens), I32)], axis=0)
    chosen = jnp.concatenate(main[0] + main[1] + edge, axis=0)
    filled = dot(chosen, jnp.ones((tokens, LANES), BF16))
    mark = jnp.where(iota(filled.shape, 1) == 0, EMPTY * (1.0 - filled), 0.0)

    def store(column, part):
        for head in range(heads):
            rows = slice(head * ROUNDS * tall, (head + 1) * ROUNDS * tall)
            send_ref[rows, column * HEAD_DIM : (column + 1) * HEAD_DIM] = part[
                :, head * HEAD_DIM : (head + 1) * HEAD_DIM
            ].astype(BF16)

    both = ROUNDS * tall
    edges = []
    for unit in range(4):
        rows = chosen if unit >= 2 else chosen[: HALVES * both]
        part = dot(rows, held_ref[:, unit * width : (unit + 1) * width])
        if unit == 0:
            part = part + jnp.concatenate([mark[: HALVES * both]] * heads, axis=1)
        for half in range(HALVES):
            store(half * 4 + unit, part[half * both : (half + 1) * both])
        edges.append(part[HALVES * both :])
    upper = (iota(edges[2].shape, 0) & CAP) == 0
    mark = jnp.concatenate([mark[HALVES * both :]] * heads, axis=1)
    store(HALVES * 4, jnp.where(upper, edges[2], edges[3]) + mark)


def unpack_kernel(n, recv_ref, rows_ref, front_ref, head_ref, info_ref):
    flat = n * SLOTS
    wide = 4 * HEAD_DIM
    lead = hot(iota((8, LANES), 1) == 0)
    row = iota((8, flat), 0)
    mine = jnp.zeros((8, flat), F32)
    for block in range(HALVES + 1):
        first = dot_nt(lead, recv_ref[:, block * wide : block * wide + LANES])
        mine = jnp.where(((row >> 1) == block) & (first < EMPTY - 1.0), 1.0, mine)
    mine = jnp.where(((iota((8, flat), 1) >> 2) & 1) == (row & 1), mine, 0.0)
    code = ranked(mine)
    at = iota((flat, LANES), 0)
    lane = iota((flat, LANES), 1)
    origin = jnp.where(lane == 0, at >> 3, jnp.where(lane == 1, at & 7, 0))
    origin = origin.astype(F32).astype(BF16)
    for half in range(HALVES):
        here = slice(half * 2 * SPAN, (half + 1) * 2 * SPAN)
        chosen = jnp.concatenate(
            [hot_rows(code[half * 2 + span : half * 2 + span + 1]) for span in range(2)], axis=0
        )
        rows = dot(chosen, recv_ref[:, half * wide : (half + 1) * wide]).astype(BF16)
        rows_ref[here, :] = rows
        info = jnp.transpose(dot(chosen, origin))[:8]
        info_ref[:, here] = info
        if half == 0:
            head_ref[:SPAN, :] = rows[:SPAN, : 2 * HEAD_DIM]
            head_ref[SPAN:, :] = jnp.concatenate(
                [info[:, :SPAN], jnp.zeros((8, SPAN), F32)], axis=0
            ).astype(BF16)
    for kind in range(2):
        chosen = hot_rows(code[2 * HALVES + kind : 2 * HALVES + kind + 1])
        front_ref[kind * SPAN : (kind + 1) * SPAN, :] = dot(
            chosen, recv_ref[:, HALVES * wide : HALVES * wide + LANES]
        ).astype(BF16)


def unit_of(ref, span, unit):
    return ref[span * SPAN : (span + 1) * SPAN, unit * HEAD_DIM : (unit + 1) * HEAD_DIM]


def forward_kernel(n, rows_ref, front_ref, info_ref, table_ref, stats_ref):
    stats_ref[...] = jnp.zeros(stats_ref.shape, F32)
    for span in range(GROUP):
        q, g, k, v = (unit_of(rows_ref, span, unit) for unit in range(4))
        if span == 0:
            k_front, v_front = unit_of(front_ref, 0, 0), unit_of(front_ref, 1, 0)
        else:
            k_front, v_front = unit_of(rows_ref, span - 1, 2), unit_of(rows_ref, span - 1, 3)
        score = dot_nt(k, q) * SCALE
        score_front = dot_nt(k_front, q) * SCALE
        highest = jnp.maximum(
            jnp.max(score, axis=0, keepdims=True), jnp.max(score_front, axis=0, keepdims=True)
        )
        raised = jnp.exp(score - highest)
        raised_front = jnp.exp(score_front - highest)
        total = jnp.sum(raised + raised_front, axis=0, keepdims=True)
        mixed = jnp.sum(
            raised * dot_nt(v, g) + raised_front * dot_nt(v_front, g), axis=0, keepdims=True
        )
        here = slice(span * SPAN, (span + 1) * SPAN)
        stats_ref[0:1, here] = highest + jnp.log(total)
        stats_ref[1:2, here] = mixed / total
    places = stats_ref.shape[1]
    slot = iota((SLOTS, places), 0) == info_ref[1:2, :].astype(I32)
    upper = iota((SLOTS, places), 1) >= 2 * SPAN
    spread = [
        jnp.where(slot & (upper == (half == 1)), stats_ref[kind : kind + 1, :], 0.0)
        for kind in range(2)
        for half in range(HALVES)
    ]
    spread.append(jnp.zeros((LANES - len(spread) * SLOTS, places), F32))
    spread = jnp.concatenate(spread, axis=0)
    owner = hot_rows(info_ref[0:1, :], n)
    table_ref[...] = sum(dot_nt(owner, part.astype(BF16)) for part in three_parts(spread))


def home_kernel(n, heads, table_ref, slots_ref, back_ref):
    tokens = slots_ref.shape[1]
    wide = GROUP * CAP
    groups = n // GROUP
    values = jnp.transpose(table_ref[...])[: 2 * wide]
    lane = iota((wide, tokens), 0)
    span_slot = []
    logs = []
    dots = []
    for turn in range(ROUNDS):
        slot = slots_ref[turn : turn + 1, :]
        group = slot >> 4
        keep = lane == (slot & 15)
        span_slot.append((group, keep, slot))
        for head in range(heads):
            member = hot_rows((head * ROUNDS + turn) * groups + group, n)
            here = picked(values, member, dot)
            logs.append(jnp.sum(jnp.where(keep, here[:wide], 0.0), axis=0, keepdims=True))
            dots.append(jnp.sum(jnp.where(keep, here[wide:], 0.0), axis=0, keepdims=True))
    members = []
    values = []
    for head in range(heads):
        log_0, log_1 = logs[head], logs[heads + head]
        highest = jnp.maximum(log_0, log_1)
        raised = [jnp.exp(log_0 - highest), jnp.exp(log_1 - highest)]
        total = raised[0] + raised[1]
        shares = [raised[0] / total, raised[1] / total]
        mean = shares[0] * dots[head] + shares[1] * dots[heads + head]
        for turn in range(ROUNDS):
            group, keep, slot = span_slot[turn]
            first = (head * ROUNDS + turn) * groups
            members.append(hot_rows(first + group, n))
            values.append(
                jnp.concatenate(
                    [jnp.where(keep, x, 0.0) for x in (shares[turn], mean)]
                    + [jnp.zeros((LANES - 2 * wide, tokens), F32)],
                    axis=0,
                )
            )
            members.append(hot_rows(first + ((group + groups - 1) & (groups - 1)), n))
            edge = iota((SLOTS, tokens), 0) == jnp.where((slot & 12) == 0, slot & 3, -1)
            values.append(
                jnp.concatenate(
                    [jnp.zeros((2 * wide, tokens), F32)]
                    + [jnp.where(edge, x, 0.0) for x in (shares[turn], mean, logs[turn * heads + head])]
                    + [jnp.zeros((LANES - 2 * wide - 3 * SLOTS, tokens), F32)],
                    axis=0,
                )
            )
    left = jnp.concatenate(members, axis=1)
    right = jnp.concatenate(values, axis=1)
    back_ref[...] = sum(dot_nt(left, part.astype(BF16)) for part in three_parts(right))


def backward_kernel(
    n, rows_ref, front_ref, behind_ref, info_ref, stats_ref, back_ref, send_ref, grads_ref
):
    flat = n * SLOTS
    places = info_ref.shape[1]
    values = jnp.transpose(back_ref[...])
    source = info_ref[0:1, :].astype(I32)
    slot = info_ref[1:2, :].astype(I32)
    keep = iota((SLOTS, places), 0) == slot
    upper = iota((SLOTS, places), 1) >= 2 * SPAN
    here = picked(values[: 4 * SLOTS], hot_rows(source, n), dot)
    own = []
    for kind in range(2):
        low = here[2 * kind * SLOTS : (2 * kind + 1) * SLOTS]
        high = here[(2 * kind + 1) * SLOTS : (2 * kind + 2) * SLOTS]
        own.append(
            jnp.sum(jnp.where(keep, jnp.where(upper, high, low), 0.0), axis=0, keepdims=True)
        )
    info = behind_ref[SPAN:, :].astype(F32).astype(I32)
    here = picked(values[4 * SLOTS : 7 * SLOTS], hot_rows(info[0:1], n), dot)
    keep = iota((SLOTS, SPAN), 0) == info[1:2]
    other = [
        jnp.sum(jnp.where(keep, here[i * SLOTS : (i + 1) * SLOTS], 0.0), axis=0, keepdims=True)
        for i in range(3)
    ]

    def graded(keys, vals, queries, grads, log_total, share, mean):
        weighted = jnp.exp(dot_nt(keys, queries) * SCALE - log_total) * share
        grad_score = weighted * ((dot_nt(vals, grads) - mean) * SCALE)
        return weighted.astype(BF16), grad_score.astype(BF16)

    def put(span, unit, grad):
        grads_ref[span * SPAN : (span + 1) * SPAN, unit * HEAD_DIM : (unit + 1) * HEAD_DIM] = (
            grad.astype(BF16)
        )

    grad_k = None
    grad_v = None
    for span in range(GROUP):
        q, g, k, v = (unit_of(rows_ref, span, unit) for unit in range(4))
        here = slice(span * SPAN, (span + 1) * SPAN)
        if span == 0:
            k_front, v_front = unit_of(front_ref, 0, 0), unit_of(front_ref, 1, 0)
        else:
            k_front, v_front = unit_of(rows_ref, span - 1, 2), unit_of(rows_ref, span - 1, 3)
        row = (stats_ref[0:1, here], own[0][:, here], own[1][:, here])
        weight, scaled = graded(k, v, q, g, *row)
        weight_front, scaled_front = graded(k_front, v_front, q, g, *row)
        put(span, 0, dot_tn(scaled, k) + dot_tn(scaled_front, k_front))
        if span > 0:
            put(span - 1, 1, grad_k + dot(scaled_front, q))
            put(span - 1, 2, grad_v + dot(weight_front, g))
        grad_k = dot(scaled, q)
        grad_v = dot(weight, g)
    q, g = behind_ref[:SPAN, :HEAD_DIM], behind_ref[:SPAN, HEAD_DIM:]
    weight, scaled = graded(k, v, q, g, other[2], other[0], other[1])
    put(GROUP - 1, 1, grad_k + dot(scaled, q))
    put(GROUP - 1, 2, grad_v + dot(weight, g))
    wide = 3 * HEAD_DIM
    slot = source * SLOTS + slot
    for half in range(HALVES):
        here = slice(half * 2 * SPAN, (half + 1) * 2 * SPAN)
        for start in range(0, flat, SPAN):
            at = slot[:, here]
            across = hot_rows(jnp.where((at >= start) & (at < start + SPAN), at - start, -1))
            send_ref[start : start + SPAN, half * wide : (half + 1) * wide] = dot(
                across, grads_ref[here, :]
            ).astype(BF16)


def final_kernel(n, slots_ref, ret_ref, dq_ref, dk_ref, dv_ref):
    tall = n // GROUP * SLOTS
    both = ROUNDS * tall
    wide = 3 * HEAD_DIM
    slots = jnp.transpose(slots_ref[...].astype(F32)).astype(I32)
    at = iota((slots.shape[0], tall), 1)
    chosen = []
    for half in range(HALVES):
        for turn in range(ROUNDS):
            slot = slots[:, turn : turn + 1]
            row = (slot >> 4) * SLOTS + (slot & 7)
            chosen.append(hot(at == jnp.where(((slot >> 3) & 1) == half, row, -1)))
    chosen = [jnp.concatenate(chosen[i * 2 : i * 2 + 2], axis=1) for i in range(HALVES)]
    for head in range(dq_ref.shape[1] // HEAD_DIM):
        rows = slice(head * both, (head + 1) * both)
        total = dot(chosen[0], ret_ref[rows, :wide]) + dot(chosen[1], ret_ref[rows, wide:])
        for unit, ref in enumerate((dq_ref, dk_ref, dv_ref)):
            ref[:, head * HEAD_DIM : (head + 1) * HEAD_DIM] = total[
                :, unit * HEAD_DIM : (unit + 1) * HEAD_DIM
            ].astype(BF16)


def call(kernel, out, name, scratch=()):
    return pl.pallas_call(
        kernel,
        out_shape=out,
        scratch_shapes=scratch,
        name=name,
        compiler_params=pltpu.CompilerParams(vmem_limit_bytes=24 * 1024 * 1024),
    )


def shape(*dims, dtype=BF16):
    return jax.ShapeDtypeStruct(dims, dtype)


def exchanged(block):
    return lax.all_to_all(block, "seq", split_axis=0, concat_axis=0, tiled=True)


def from_next_group(block):
    n = lax.axis_size("seq")
    groups = n // GROUP
    route = [(i // groups * groups + (i + 1) % groups, i) for i in range(n)]
    return lax.ppermute(block, "seq", route)


def body(queries, keys, values, out_grad, sorted_position):
    n = lax.axis_size("seq")
    tokens, width = queries.shape
    heads = width // HEAD_DIM
    flat = n * SLOTS
    places = GROUP * SPAN
    placed = lax.all_gather(sorted_position, "head", axis=0, tiled=True)
    send, slots = call(
        functools.partial(pack_kernel, n),
        (shape(flat, (4 * HALVES + 1) * HEAD_DIM), shape(8, tokens, dtype=I32)),
        "pack",
    )(placed, jnp.concatenate([queries, out_grad, keys, values], axis=1))
    rows, front, first, info = call(
        functools.partial(unpack_kernel, n),
        (
            shape(places, 4 * HEAD_DIM),
            shape(2 * SPAN, HEAD_DIM),
            shape(SPAN + 16, 2 * HEAD_DIM),
            shape(8, places, dtype=F32),
        ),
        "unpack",
    )(exchanged(send))
    behind = from_next_group(first)
    table, stats = call(
        functools.partial(forward_kernel, n),
        (shape(n, LANES, dtype=F32), shape(8, places, dtype=F32)),
        "forward",
    )(rows, front, info)
    back = call(functools.partial(home_kernel, n, heads), shape(n, LANES, dtype=F32), "home")(
        exchanged(table), slots
    )
    grads = call(
        functools.partial(backward_kernel, n),
        shape(flat, 3 * HALVES * HEAD_DIM),
        "backward",
        [pltpu.VMEM((places, 3 * HEAD_DIM), BF16)],
    )(rows, front, behind, info, stats, exchanged(back))
    return call(functools.partial(final_kernel, n), (shape(tokens, width),) * 3, "final")(
        slots, exchanged(grads)
    )


def solution(mesh):
    in_specs = (
        P("seq", "head"),
        P("seq", "head"),
        P("seq", "head"),
        P("seq", "head"),
        P(None, ("seq", "head")),
    )
    out_specs = (P("seq", "head"), P("seq", "head"), P("seq", "head"))
    return jax.shard_map(body, mesh=mesh, in_specs=in_specs, out_specs=out_specs, check_vma=False)
```

time: 186 us -> 184 us (0.989)
  waiting for transfers between devices: 14.6 us -> 20.2 us
  starting transfers between devices: 22.2 us -> 16.6 us
    all_to_all x2, waiting for transfers between devices: 14.6 us -> 20.2 us  [exchanged(): return lax.all_to_all(block, 'seq', split_axis=0, concat_axis=0, tiled=True)]
    ppermute x1, starting transfers between devices: 8.24 us -> 2.8 us  [from_next_group(): return lax.ppermute(block, 'seq', route)]
where the time goes in v2:
time: 184 us; the launch traced here: 183 us
  blocking collectives  132 us (72%)
  waiting for transfers between devices  20.2 us (11%)
  starting transfers between devices  16.6 us (9%)
  Pallas kernels  12.9 us (7%)
    all_to_all x2, blocking collectives, exchanged(): return lax.all_to_all(block, 'seq', split_axis=0, concat_axis=0, tiled=True)  123 us
    all_to_all x2, waiting for transfers between devices, exchanged(): return lax.all_to_all(block, 'seq', split_axis=0, concat_axis=0, tiled=True)  20.2 us
    all_to_all x2, starting transfers between devices, exchanged(): return lax.all_to_all(block, 'seq', split_axis=0, concat_axis=0, tiled=True)  13.8 us
    all_gather x1, blocking collectives, body(): placed = lax.all_gather(sorted_position, 'head', axis=0, tiled=True)  8.78 us
  transfers between devices with their start and end apart: 3, of which 2 were waited for; matrix products, arithmetic and copies ran while one was open for 0% of the time, Pallas kernels for 1%

profile of v2, /device:TPU:1, one launch (start us, length us, event | category | flops | bytes accessed | tf_op | source)
XLA Modules:
  0.0 183.4 jit_solution(4039062641551897538)
XLA Ops:
  0.6 8.8 %all-gather = s32[4,2,64]{2,1,0:T(2,128)S(1)} all-gather(s32[1,2,64]{2,1,0:T(2,128)} %bitcast.21), channel_id=1, replica_groups=mesh['seq'=128,'head'=4] {'head'}, dimensions={0}, use_global_device_ids=true | all-gather | bytes 2560 | tf_op jit(solution)/shard_map/all_gather | solution.py:392
  9.4 1.2 pad_maximum_fusion.held_ref
  10.6 1.3 pack.1
  11.9 76.9 %all_to_all.44 = bf16[128,8,1152]{2,1,0:T(8,128)(2,1)S(1)} all-to-all(bf16[128,8,1152]{2,1,0:T(8,128)(2,1)S(1)} %bitcast.17), channel_id=1, replica_groups=mesh['seq'=128,'head'=4] {'seq'}, dimensions={0} | all-to-all | bytes 4718592 | tf_op jit(solution)/shard_map/all_to_all | solution.py:376
  88.8 2.5 %unpack.1 = (bf16[1024,512]{1,0:T(8,128)(2,1)S(1)}, bf16[512,128]{1,0:T(8,128)(2,1)S(1)}, bf16[272,256]{1,0:T(8,128)(2,1)S(1)}, f32[8,1024]{1,0:T(8,128)S(1)}) custom-call(bf16[1024,1152]{1,0:T(8,128)(2,1)S(1)} %bitcast.14), custom_call_target="tpu_custom_call" | custom-call | tf_op jit(solution)/shard_map/unpack/pallas_call | solution.py:398
  91.3 2.4 %forward.1 = (f32[128,128]{1,0:T(8,128)}, f32[8,1024]{1,0:T(8,128)S(1)}) custom-call(bf16[1024,512]{1,0:T(8,128)(2,1)S(1)} %get-tuple-element.13.rows_ref, bf16[512,128]{1,0:T(8,128)(2,1)S(1)} %get-tuple-element.14.front_ref, f32[8,1024]{1,0:T(8,128)S(1)} %get-tuple-element.16.info_ref), custom_call_target="tpu_custom_call" | custom-call | tf_op jit(solution)/shard_map/forward/pallas_call | solution.py:409
  93.7 8.1 %all-to-all-start.1 = ((f32[128,1,128]{2,1,0:T(1,128)}), f32[128,1,128]{2,1,0:T(1,128)S(1)}, u32[]{:S(2)}, u32[]{:S(2)}) async-start(f32[128,1,128]{2,1,0:T(1,128)} %bitcast.5), calls=%async_computation.1 | async-start | bytes 131072 | tf_op jit(solution)/shard_map/all_to_all | solution.py:376
  101.8 2.8 %collective-permute-start = (bf16[272,256]{1,0:T(8,128)(2,1)S(1)}, bf16[272,256]{1,0:T(8,128)(2,1)S(1)}, u32[]{:S(2)}, u32[]{:S(2)}) collective-permute-start(bf16[272,256]{1,0:T(8,128)(2,1)S(1)} %get-tuple-element.15), channel_id=1, source_target_pairs={{4,0},{8,4},{12,8},{16,12},{20,16},{24,20},{28,24},{32,28},{36,32}... | collective-permute-start | bytes 417800 | tf_op jit(solution)/shard_map/ppermute | solution.py:383
  104.6 8.6 %all-to-all-done.1 = f32[128,1,128]{2,1,0:T(1,128)S(1)} async-done(((f32[128,1,128]{2,1,0:T(1,128)}), f32[128,1,128]{2,1,0:T(1,128)S(1)}, u32[]{:S(2)}, u32[]{:S(2)}) %all-to-all-start.1) | async-done | bytes 65568 | tf_op jit(solution)/shard_map/all_to_all | solution.py:376
  113.2 1.5 home.1
  114.7 5.7 %all-to-all-start.2 = ((f32[128,1,128]{2,1,0:T(1,128)}), f32[128,1,128]{2,1,0:T(1,128)S(1)}, u32[]{:S(2)}, u32[]{:S(2)}) async-start(f32[128,1,128]{2,1,0:T(1,128)} %bitcast.8), calls=%async_computation.2 | async-start | bytes 131072 | tf_op jit(solution)/shard_map/all_to_all | solution.py:376
  120.4 0.0 collective-permute-done.behind_ref
  120.4 11.5 %all-to-all-done.2 = f32[128,1,128]{2,1,0:T(1,128)S(1)} async-done(((f32[128,1,128]{2,1,0:T(1,128)}), f32[128,1,128]{2,1,0:T(1,128)S(1)}, u32[]{:S(2)}, u32[]{:S(2)}) %all-to-all-start.2) | async-done | bytes 65568 | tf_op jit(solution)/shard_map/all_to_all | solution.py:376
  132.0 3.6 %backward.1 = bf16[1024,768]{1,0:T(8,128)(2,1)S(1)} custom-call(bf16[1024,512]{1,0:T(8,128)(2,1)S(1)} %get-tuple-element.13.rows_ref, bf16[512,128]{1,0:T(8,128)(2,1)S(1)} %get-tuple-element.14.front_ref, bf16[272,256]{1,0:T(8,128)(2,1)S(1)} %collective-permute-done.behind_ref, f32[8,1024]{1,0:T(8,128)S(1)} %get-tuple-element.16.info_ref, ...), custom_call_target="tpu_custom_call" | custom-call | tf_op jit(solution)/shard_map/backward/pallas_call | solution.py:417
  135.6 46.1 %all_to_all.45 = bf16[128,8,768]{2,1,0:T(8,128)(2,1)S(1)} all-to-all(bf16[128,8,768]{2,1,0:T(8,128)(2,1)S(1)} %bitcast.15), channel_id=1, replica_groups=mesh['seq'=128,'head'=4] {'seq'}, dimensions={0} | all-to-all | bytes 3145728 | tf_op jit(solution)/shard_map/all_to_all | solution.py:376
  181.7 1.6 final.1
Async XLA Ops:
  93.7 19.6 %all-to-all-start.1 = ((f32[128,1,128]{2,1,0:T(1,128)}), f32[128,1,128]{2,1,0:T(1,128)S(1)}, u32[]{:S(2)}, u32[]{:S(2)}) async-start(f32[128,1,128]{2,1,0:T(1,128)} %bitcast.5), calls=%async_computation.1 | async-start | bytes 131072 | tf_op jit(solution)/shard_map/all_to_all | solution.py:376
  101.8 18.6 %collective-permute-start = (bf16[272,256]{1,0:T(8,128)(2,1)S(1)}, bf16[272,256]{1,0:T(8,128)(2,1)S(1)}, u32[]{:S(2)}, u32[]{:S(2)}) collective-permute-start(bf16[272,256]{1,0:T(8,128)(2,1)S(1)} %get-tuple-element.15), channel_id=1, source_target_pairs={{4,0},{8,4},{12,8},{16,12},{20,16},{24,20},{28,24},{32,28},{36,32}... | collective-permute-start | bytes 417800 | tf_op jit(solution)/shard_map/ppermute | solution.py:383
  114.7 17.3 %all-to-all-start.2 = ((f32[128,1,128]{2,1,0:T(1,128)}), f32[128,1,128]{2,1,0:T(1,128)S(1)}, u32[]{:S(2)}, u32[]{:S(2)}) async-start(f32[128,1,128]{2,1,0:T(1,128)} %bitcast.8), calls=%async_computation.2 | async-start | bytes 131072 | tf_op jit(solution)/shard_map/all_to_all | solution.py:376

commit v3 on v2

v3 whole, which is shorter than its diff:
```python
import functools
import math

import jax
import jax.numpy as jnp
from jax import lax
from jax.experimental import pallas as pl
from jax.experimental.pallas import tpu as pltpu
from jax.sharding import PartitionSpec as P

HEAD_DIM = 128
SPAN = 256
ROUNDS = 2
CAP = 4
GROUP = 4
SLOTS = 8
HALVES = 2
LANES = 128
DUP_LANE = 16
SOURCE_LANE = 20
NOTES = 24
SCALE = 1.0 / math.sqrt(HEAD_DIM)
F32 = jnp.float32
BF16 = jnp.bfloat16
I32 = jnp.int32


def iota(shape, dim):
    return lax.broadcasted_iota(I32, shape, dim)


def hot(condition):
    return jnp.where(condition, 1.0, 0.0).astype(BF16)


def dot(a, b):
    return lax.dot_general(a, b, (((1,), (0,)), ((), ())), preferred_element_type=F32)


def dot_nt(a, b):
    return lax.dot_general(a, b, (((1,), (1,)), ((), ())), preferred_element_type=F32)


def dot_tn(a, b):
    return lax.dot_general(a, b, (((0,), (0,)), ((), ())), preferred_element_type=F32)


def three_parts(x):
    high = x.astype(BF16).astype(F32)
    rest = x - high
    middle = rest.astype(BF16).astype(F32)
    return high, middle, (rest - middle).astype(BF16).astype(F32)


def picked(x, onehot, product):
    rows = x.shape[0]
    stacked = jnp.concatenate(three_parts(x), axis=0).astype(BF16)
    out = product(stacked, onehot)
    return out[:rows] + out[rows : 2 * rows] + out[2 * rows :]


def hot_rows(code, rows=SPAN):
    at = iota((rows, LANES), 0).astype(F32).astype(BF16)
    code = code.astype(F32).astype(BF16)
    pieces = [
        jnp.where(at == code[:, i : i + LANES], jnp.ones_like(at), jnp.zeros_like(at))
        for i in range(0, code.shape[1], LANES)
    ]
    return jnp.concatenate(pieces, axis=1)


def pack_kernel(n, pos_ref, held_ref, send_ref, slots_ref):
    tokens = held_ref.shape[0]
    width = held_ref.shape[1] // 4
    heads = width // HEAD_DIM
    quarters = pos_ref.shape[0] // ROUNDS
    tall = n // GROUP * SLOTS
    before = hot(iota((tokens, tokens), 0) < iota((tokens, tokens), 1))
    main = [[], []]
    edge = []
    notes = []
    slots = []
    all_places = [
        jnp.concatenate(
            [pos_ref[x * ROUNDS + turn : x * ROUNDS + turn + 1, :] for x in range(quarters)], axis=1
        )
        for turn in range(ROUNDS)
    ]
    lane = iota((LANES, tokens), 0)
    for turn in range(ROUNDS):
        places = all_places[turn]
        other = all_places[1 - turn]
        span = places >> 8
        inner = span & 3
        member = hot_rows(span, n)
        earlier = dot(member, before)
        rank = jnp.sum(member.astype(F32) * earlier, axis=0, keepdims=True).astype(I32)
        slots.append(span * CAP + rank)
        row = (span >> 2) * SLOTS + rank
        for half in range(HALVES):
            here = (inner >> 1) == half
            main[half].append(hot_rows(jnp.where(here, row + (inner & 1) * CAP, -1)))
        last = (span & 7) == 7
        first = (((span + 1) & (n - 1)) >> 2) * SLOTS + rank
        edge.append([hot_rows(jnp.where(last, first + i * SLOTS, -1)) for i in range(2)])
        landing = (places & 255) + 1
        values = jnp.where(lane == inner * 4, landing, 0)
        values = jnp.where(lane == inner * 4 + 1, other >> 7, values)
        values = jnp.where(lane == inner * 4 + 2, other & 127, values)
        note = dot_nt(hot_rows(row + CAP), values.astype(F32).astype(BF16))
        values = jnp.where(lane == DUP_LANE, landing, 0).astype(F32).astype(BF16)
        both = [hot_rows(jnp.where(last, first + i * SLOTS + CAP, -1)) for i in range(2)]
        notes.append(note + dot_nt(both[0] + both[1], values))
    slots_ref[...] = jnp.concatenate(slots + [jnp.zeros((8 - ROUNDS, tokens), I32)], axis=0)
    chosen = jnp.concatenate(main[0] + main[1], axis=0)

    def store(column, part):
        for head in range(heads):
            rows = slice(head * ROUNDS * tall, (head + 1) * ROUNDS * tall)
            send_ref[rows, column * HEAD_DIM : (column + 1) * HEAD_DIM] = part[
                :, head * HEAD_DIM : (head + 1) * HEAD_DIM
            ].astype(BF16)

    both = ROUNDS * tall
    for unit in range(4):
        part = dot(chosen, held_ref[:, unit * width : (unit + 1) * width])
        for half in range(HALVES):
            store(half * 4 + unit, part[half * both : (half + 1) * both])
    extra = dot(jnp.concatenate([edge[0][0], edge[1][0]], axis=0), held_ref[:, 2 * width : 3 * width])
    extra = extra + dot(
        jnp.concatenate([edge[0][1], edge[1][1]], axis=0), held_ref[:, 3 * width :]
    )
    notes = jnp.concatenate(notes, axis=0)
    store(HALVES * 4, extra + jnp.concatenate([notes] * heads, axis=1))


def unpack_kernel(n, me_ref, recv_ref, rows_ref, dup_ref, pair_ref, head_ref, info_ref):
    flat = n * SLOTS
    wide = 4 * HEAD_DIM
    odd = (me_ref[0] & 1) == 1
    extra = recv_ref[:, HALVES * wide :]
    at = iota((flat, LANES), 0)
    lane = iota((flat, LANES), 1)
    notes = extra.astype(F32)
    notes = jnp.where((at & 7) < CAP, pltpu.roll(notes, flat - CAP, 0), notes)
    notes = jnp.where(lane == SOURCE_LANE, (at >> 3).astype(F32), notes)
    notes = jnp.where(lane == SOURCE_LANE + 1, (at & 7).astype(F32), notes).astype(BF16)
    by_slot = dot_nt(hot(iota((NOTES, LANES), 0) == iota((NOTES, LANES), 1)), notes).astype(I32)
    upper = (iota((1, flat), 1) & 7) >= CAP
    for half in range(HALVES):
        here = slice(half * 2 * SPAN, (half + 1) * 2 * SPAN)
        chosen = []
        for i in range(2):
            row = (half * 2 + i) * 4
            chosen.append(hot_rows(jnp.where(upper == (i == 1), by_slot[row : row + 1] - 1, -1)))
        chosen = jnp.concatenate(chosen, axis=0)
        rows = dot(chosen, recv_ref[:, half * wide : (half + 1) * wide]).astype(BF16)
        rows_ref[here, :] = rows
        by_place = jnp.transpose(dot(chosen, notes))[:NOTES]
        row = half * 8
        away = [
            jnp.concatenate(
                [by_place[row + i : row + i + 1, :SPAN], by_place[row + i + 4 : row + i + 5, SPAN:]],
                axis=1,
            )
            for i in (1, 2)
        ]
        info = jnp.concatenate(
            away
            + [by_place[SOURCE_LANE : SOURCE_LANE + 2], jnp.zeros((4, 2 * SPAN), F32)],
            axis=0,
        )
        info_ref[:, here] = info
        if half == 0:
            head_ref[:SPAN, :] = rows[:SPAN, : 2 * HEAD_DIM]
            head_ref[SPAN:, :] = jnp.concatenate(
                [info[:, :SPAN], jnp.zeros((8, SPAN), F32)], axis=0
            ).astype(BF16)
    chosen = hot_rows(jnp.where(upper, -1, by_slot[DUP_LANE : DUP_LANE + 1] - 1))
    dup = dot(chosen, extra)
    dup_ref[...] = dup.astype(BF16)
    dup = jnp.concatenate([dup, jnp.zeros_like(dup)], axis=1)
    last = rows_ref[(GROUP - 1) * SPAN :, 2 * HEAD_DIM :].astype(F32)
    pair_ref[...] = jnp.where(odd, dup, last).astype(BF16)


def before_group(odd, dup_ref, pair_ref):
    k_even, v_even = pair_ref[:SPAN, :HEAD_DIM], pair_ref[:SPAN, HEAD_DIM:]
    k_front = jnp.where(odd, k_even.astype(F32), dup_ref[...].astype(F32))
    v_front = jnp.where(odd, v_even.astype(F32), pair_ref[SPAN:, :HEAD_DIM].astype(F32))
    return k_front.astype(BF16), v_front.astype(BF16)


def unit_of(ref, span, unit):
    return ref[span * SPAN : (span + 1) * SPAN, unit * HEAD_DIM : (unit + 1) * HEAD_DIM]


def forward_kernel(me_ref, rows_ref, dup_ref, pair_ref, table_ref, stats_ref):
    front = before_group((me_ref[0] & 1) == 1, dup_ref, pair_ref)
    for span in range(GROUP):
        q, g, k, v = (unit_of(rows_ref, span, unit) for unit in range(4))
        if span == 0:
            k_front, v_front = front
        else:
            k_front, v_front = unit_of(rows_ref, span - 1, 2), unit_of(rows_ref, span - 1, 3)
        score = dot_nt(k, q) * SCALE
        score_front = dot_nt(k_front, q) * SCALE
        highest = jnp.maximum(
            jnp.max(score, axis=0, keepdims=True), jnp.max(score_front, axis=0, keepdims=True)
        )
        raised = jnp.exp(score - highest)
        raised_front = jnp.exp(score_front - highest)
        total = jnp.sum(raised + raised_front, axis=0, keepdims=True)
        mixed = jnp.sum(
            raised * dot_nt(v, g) + raised_front * dot_nt(v_front, g), axis=0, keepdims=True
        )
        here = slice(span * SPAN, (span + 1) * SPAN)
        for kind, row in enumerate((highest + jnp.log(total), mixed / total)):
            stats_ref[kind : kind + 1, here] = row
            for i in range(2):
                at = kind * SLOTS + span * 2 + i
                table_ref[at : at + 1, :] = row[:, i * LANES : (i + 1) * LANES]
    stats_ref[2:, :] = jnp.zeros((6, GROUP * SPAN), F32)


def backward_kernel(
    n,
    me_ref,
    rows_ref,
    dup_ref,
    pair_ref,
    behind_ref,
    info_ref,
    stats_ref,
    table_ref,
    send_ref,
    grads_ref,
):
    flat = n * SLOTS
    groups = n // GROUP
    me = me_ref[0]
    turn = (me >> 5) & 1
    group = (me + 1) & (groups - 1)
    behind_info = behind_ref[SPAN : SPAN + 8, :].astype(F32)
    far = jnp.concatenate([info_ref[0:1, :], behind_info[0:1]], axis=1).astype(I32)
    near = jnp.concatenate([info_ref[1:2, :], behind_info[1:2]], axis=1).astype(I32)
    chosen = hot_rows(((far >> 3) & 15) * 16 + (far >> 7) * 8 + (far & 7))
    keep = iota((LANES, far.shape[1]), 0) == near

    def tile(turn, high, kind):
        return pl.ds(pl.multiple_of(turn * 32 + high * 16 + kind * 8, 8), 8)

    there = []
    own = []
    for kind in range(2):
        tiles = [table_ref[:, tile(1 - turn, high, kind), :] for high in range(2)]
        there.append(jnp.transpose(jnp.concatenate(tiles, axis=1).reshape(2 * LANES, LANES)))
        next_tile = table_ref[group & 15, tile(turn, group >> 4, kind), :]
        own.append(
            jnp.concatenate([stats_ref[kind : kind + 1, :], next_tile[0:1], next_tile[1:2]], axis=1)
        )
    found = picked(jnp.concatenate(there, axis=0), chosen, dot)
    other = [
        jnp.sum(
            jnp.where(keep, found[kind * LANES : (kind + 1) * LANES], 0.0), axis=0, keepdims=True
        )
        for kind in range(2)
    ]
    highest = jnp.maximum(own[0], other[0])
    raised = jnp.exp(own[0] - highest)
    raised_other = jnp.exp(other[0] - highest)
    total = raised + raised_other
    shares = raised / total
    means = (raised * own[1] + raised_other * other[1]) / total

    def graded(keys, vals, queries, grads, log_total, share, mean):
        weighted = jnp.exp(dot_nt(keys, queries) * SCALE - log_total) * share
        grad_score = weighted * ((dot_nt(vals, grads) - mean) * SCALE)
        return weighted.astype(BF16), grad_score.astype(BF16)

    def put(span, unit, grad):
        grads_ref[span * SPAN : (span + 1) * SPAN, unit * HEAD_DIM : (unit + 1) * HEAD_DIM] = (
            grad.astype(BF16)
        )

    grad_k = None
    grad_v = None
    for span in range(GROUP):
        q, g, k, v = (unit_of(rows_ref, span, unit) for unit in range(4))
        here = slice(span * SPAN, (span + 1) * SPAN)
        if span == 0:
            k_front, v_front = before_group((me & 1) == 1, dup_ref, pair_ref)
        else:
            k_front, v_front = unit_of(rows_ref, span - 1, 2), unit_of(rows_ref, span - 1, 3)
        row = (own[0][:, here], shares[:, here], means[:, here])
        weight, scaled = graded(k, v, q, g, *row)
        weight_front, scaled_front = graded(k_front, v_front, q, g, *row)
        put(span, 0, dot_tn(scaled, k) + dot_tn(scaled_front, k_front))
        if span > 0:
            put(span - 1, 1, grad_k + dot(scaled_front, q))
            put(span - 1, 2, grad_v + dot(weight_front, g))
        grad_k = dot(scaled, q)
        grad_v = dot(weight, g)
    here = slice(GROUP * SPAN, (GROUP + 1) * SPAN)
    q, g = behind_ref[:SPAN, :HEAD_DIM], behind_ref[:SPAN, HEAD_DIM:]
    weight, scaled = graded(k, v, q, g, own[0][:, here], shares[:, here], means[:, here])
    put(GROUP - 1, 1, grad_k + dot(scaled, q))
    put(GROUP - 1, 2, grad_v + dot(weight, g))
    wide = 3 * HEAD_DIM
    slot = (info_ref[2:3, :] * SLOTS + info_ref[3:4, :]).astype(I32)
    for half in range(HALVES):
        here = slice(half * 2 * SPAN, (half + 1) * 2 * SPAN)
        for start in range(0, flat, SPAN):
            at = slot[:, here]
            across = hot_rows(jnp.where((at >= start) & (at < start + SPAN), at - start, -1))
            send_ref[start : start + SPAN, half * wide : (half + 1) * wide] = dot(
                across, grads_ref[here, :]
            ).astype(BF16)


def final_kernel(n, slots_ref, ret_ref, dq_ref, dk_ref, dv_ref):
    tall = n // GROUP * SLOTS
    both = ROUNDS * tall
    wide = 3 * HEAD_DIM
    slots = jnp.transpose(slots_ref[...].astype(F32)).astype(I32)
    at = iota((slots.shape[0], tall), 1)
    chosen = []
    for half in range(HALVES):
        for turn in range(ROUNDS):
            slot = slots[:, turn : turn + 1]
            row = (slot >> 4) * SLOTS + (slot & 7)
            chosen.append(hot(at == jnp.where(((slot >> 3) & 1) == half, row, -1)))
    chosen = [jnp.concatenate(chosen[i * 2 : i * 2 + 2], axis=1) for i in range(HALVES)]
    for head in range(dq_ref.shape[1] // HEAD_DIM):
        rows = slice(head * both, (head + 1) * both)
        total = dot(chosen[0], ret_ref[rows, :wide]) + dot(chosen[1], ret_ref[rows, wide:])
        for unit, ref in enumerate((dq_ref, dk_ref, dv_ref)):
            ref[:, head * HEAD_DIM : (head + 1) * HEAD_DIM] = total[
                :, unit * HEAD_DIM : (unit + 1) * HEAD_DIM
            ].astype(BF16)


def call(kernel, out, name, args, scratch=()):
    where = [pltpu.SMEM if x.shape == (1,) else pltpu.VMEM for x in args]
    return pl.pallas_call(
        kernel,
        out_shape=out,
        in_specs=[pl.BlockSpec(memory_space=space) for space in where],
        scratch_shapes=scratch,
        name=name,
        compiler_params=pltpu.CompilerParams(vmem_limit_bytes=24 * 1024 * 1024),
    )(*args)


def shape(*dims, dtype=BF16):
    return jax.ShapeDtypeStruct(dims, dtype)


def exchanged(block):
    return lax.all_to_all(block, "seq", split_axis=0, concat_axis=0, tiled=True)


def gathered(block, members):
    n = lax.axis_size("seq")
    taken = set()
    groups = []
    for first in range(n):
        if first not in taken:
            groups.append([first + offset for offset in members])
            taken.update(groups[-1])
    return lax.all_gather(block, "seq", axis=0, tiled=True, axis_index_groups=groups)


def from_next_group(block):
    n = lax.axis_size("seq")
    groups = n // GROUP
    route = [(i // groups * groups + (i + 1) % groups, i) for i in range(n)]
    return lax.ppermute(block, "seq", route)


def body(queries, keys, values, out_grad, sorted_position):
    n = lax.axis_size("seq")
    tokens, width = queries.shape
    flat = n * SLOTS
    places = GROUP * SPAN
    me = lax.axis_index("seq").astype(I32).reshape(1)
    placed = lax.all_gather(sorted_position, "head", axis=0, tiled=True)
    send, slots = call(
        functools.partial(pack_kernel, n),
        (shape(flat, (4 * HALVES + 1) * HEAD_DIM), shape(8, tokens, dtype=I32)),
        "pack",
        (placed, jnp.concatenate([queries, out_grad, keys, values], axis=1)),
    )
    send, me = lax.optimization_barrier((send, me))
    rows, dup, last, first, info = call(
        functools.partial(unpack_kernel, n),
        (
            shape(places, 4 * HEAD_DIM),
            shape(SPAN, HEAD_DIM),
            shape(SPAN, 2 * HEAD_DIM),
            shape(SPAN + 16, 2 * HEAD_DIM),
            shape(8, places, dtype=F32),
        ),
        "unpack",
        (me, exchanged(send)),
    )
    behind = from_next_group(first)
    pair = gathered(last, (0, 1))
    table, stats = call(
        forward_kernel,
        (shape(2 * SLOTS, LANES, dtype=F32), shape(8, places, dtype=F32)),
        "forward",
        (me, rows, dup, pair),
    )
    for members in ((0, n // 8), (0, n // 4), range(n // 8)):
        table = gathered(table, members)
    grads = call(
        functools.partial(backward_kernel, n),
        shape(flat, 3 * HALVES * HEAD_DIM),
        "backward",
        (me, rows, dup, pair, behind, info, stats, table.reshape(n // 8, 4 * 2 * SLOTS, LANES)),
        [pltpu.VMEM((places, 3 * HEAD_DIM), BF16)],
    )
    return call(
        functools.partial(final_kernel, n),
        (shape(tokens, width),) * 3,
        "final",
        (slots, exchanged(grads)),
    )


def solution(mesh):
    in_specs = (
        P("seq", "head"),
        P("seq", "head"),
        P("seq", "head"),
        P("seq", "head"),
        P(None, ("seq", "head")),
    )
    out_specs = (P("seq", "head"), P("seq", "head"), P("seq", "head"))
    return jax.shard_map(body, mesh=mesh, in_specs=in_specs, out_specs=out_specs, check_vma=False)
```

time: 184 us -> 179 us (0.973)
  blocking collectives: 132 us -> 162 us
  waiting for transfers between devices: 20.2 us -> 0.01 us
  starting transfers between devices: 16.6 us -> 4.56 us
  Pallas kernels: 12.9 us -> 10.1 us
    all_gather x0 -> x4, blocking collectives: none -> 27.3 us  [gathered(): lax.all_gather(block, 'seq', axis=0, tiled=True, axis_index_groups=groups)]
    all_to_all x2 -> x0, waiting for transfers between devices: 20.2 us -> none  [exchanged(): return lax.all_to_all(block, 'seq', split_axis=0, concat_axis=0, tiled=True)]
    all_to_all x2 -> x0, starting transfers between devices: 13.8 us -> none  [exchanged(): return lax.all_to_all(block, 'seq', split_axis=0, concat_axis=0, tiled=True)]
    all_to_all x2, blocking collectives: 123 us -> 126 us  [exchanged(): return lax.all_to_all(block, 'seq', split_axis=0, concat_axis=0, tiled=True)]
    pallas_call x6 -> x5, Pallas kernels: 12.9 us -> 10.1 us  [call(): pl.pallas_call(kernel, out_shape=out, in_specs=[pl.BlockSpec(memory_space...]
  transfers between devices with their start and end apart: 3 -> 1, of which waited for: 2 -> 0; matrix products, arithmetic and copies ran while one was open for 0% -> 0% of each run, Pallas kernels for 1% -> 0%
where the time goes in v3:
time: 179 us; the launch traced here: 178 us
  blocking collectives  162 us (91%)
  Pallas kernels  10.1 us (6%)
  starting transfers between devices  4.56 us (3%)
    all_to_all x2, blocking collectives, exchanged(): return lax.all_to_all(block, 'seq', split_axis=0, concat_axis=0, tiled=True)  126 us
    all_gather x4, blocking collectives, gathered(): lax.all_gather(block, 'seq', axis=0, tiled=True, axis_index_groups=groups)  27.3 us
    pallas_call x5, Pallas kernels, call(): pl.pallas_call(kernel, out_shape=out, in_specs=[pl.BlockSpec(memory_space...  10.1 us
    all_gather x1, blocking collectives, body(): placed = lax.all_gather(sorted_position, 'head', axis=0, tiled=True)  8.78 us
    ppermute x1, starting transfers between devices, from_next_group(): return lax.ppermute(block, 'seq', route)  4.56 us
  transfers between devices with their start and end apart: 1, of which 0 were waited for; matrix products, arithmetic and copies ran while one was open for 0% of the time, Pallas kernels for 0%

profile of v3, /device:TPU:1, one launch (start us, length us, event | category | flops | bytes accessed | tf_op | source)
XLA Modules:
  0.0 178.5 jit_solution(10436451177573341258)
XLA Ops:
  0.6 8.8 %all-gather = s32[4,2,64]{2,1,0:T(2,128)S(1)} all-gather(s32[1,2,64]{2,1,0:T(2,128)} %bitcast.14), channel_id=1, replica_groups=mesh['seq'=128,'head'=4] {'head'}, dimensions={0}, use_global_device_ids=true | all-gather | bytes 2560 | tf_op jit(solution)/shard_map/all_gather | solution.py:387
  9.4 1.2 pad_maximum_fusion.held_ref
  10.6 1.3 pack.1
  11.8 76.9 %all_to_all.22 = bf16[128,8,1152]{2,1,0:T(8,128)(2,1)S(1)} all-to-all(bf16[128,8,1152]{2,1,0:T(8,128)(2,1)S(1)} %bitcast.11), channel_id=1, replica_groups=mesh['seq'=128,'head'=4] {'seq'}, dimensions={0} | all-to-all | bytes 4718592 | tf_op jit(solution)/shard_map/all_to_all | solution.py:360
  88.8 2.2 %unpack.1 = (bf16[1024,512]{1,0:T(8,128)(2,1)S(1)}, bf16[256,128]{1,0:T(8,128)(2,1)S(1)}, bf16[256,256]{1,0:T(8,128)(2,1)S(1)}, bf16[272,256]{1,0:T(8,128)(2,1)S(1)}, f32[8,1024]{1,0:T(8,128)S(1)}) custom-call(s32[1]{0:T(128)} %bitcast.2.me_ref, bf16[1024,1152]{1,0:T(8,128)(2,1)S(1)} %bitcast.8), custom_call_target="tpu_custom_call" | custom-call | tf_op jit(solution)/shard_map/unpack/pallas_call | solution.py:345
  90.9 2.3 %all_gather.16.pair_ref = bf16[512,256]{1,0:T(8,128)(2,1)S(1)} all-gather(bf16[256,256]{1,0:T(8,128)(2,1)S(1)} %get-tuple-element.20), channel_id=1, replica_groups={{0,4},{8,12},{16,20},{24,28},{32,36},{40,44},{48,52},{56,60},{64,68},{7..., dimensions={0}, use_global_device_ids=true | all-gather | bytes 393216 | tf_op jit(solution)/shard_map/all_gather | solution.py:371
  93.2 1.0 forward.1
  94.2 3.2 %all_gather.17 = f32[32,128]{1,0:T(8,128)S(1)} all-gather(f32[16,128]{1,0:T(8,128)S(1)} %get-tuple-element.24), channel_id=1, replica_groups={{0,64},{4,68},{8,72},{12,76},{16,80},{20,84},{24,88},{28,92},{32,96},{3..., dimensions={0}, use_global_device_ids=true | all-gather | bytes 24576 | tf_op jit(solution)/shard_map/all_gather | solution.py:371
  97.4 4.2 %all_gather.18 = f32[64,128]{1,0:T(8,128)S(1)} all-gather(f32[32,128]{1,0:T(8,128)S(1)} %all_gather.17), channel_id=1, replica_groups={{0,128},{4,132},{8,136},{12,140},{16,144},{20,148},{24,152},{28,156},{3..., dimensions={0}, use_global_device_ids=true | all-gather | bytes 49152 | tf_op jit(solution)/shard_map/all_gather | solution.py:371
  101.6 4.6 %collective-permute-start = (bf16[272,256]{1,0:T(8,128)(2,1)S(1)}, bf16[272,256]{1,0:T(8,128)(2,1)S(1)}, u32[]{:S(2)}, u32[]{:S(2)}) collective-permute-start(bf16[272,256]{1,0:T(8,128)(2,1)S(1)} %get-tuple-element.21), channel_id=1, source_target_pairs={{4,0},{8,4},{12,8},{16,12},{20,16},{24,20},{28,24},{32,28},{36,32}... | collective-permute-start | bytes 417800 | tf_op jit(solution)/shard_map/ppermute | solution.py:378
  106.1 17.6 %all_gather.19 = f32[1024,128]{1,0:T(8,128)S(1)} all-gather(f32[64,128]{1,0:T(8,128)S(1)} %all_gather.18), channel_id=1, replica_groups={{0,4,8,12,16,20,24,28,32,36,40,44,48,52,56,60},{64,68,72,76,80,84,88,92..., dimensions={0}, use_global_device_ids=true | all-gather | bytes 557056 | tf_op jit(solution)/shard_map/all_gather | solution.py:371
  123.8 0.0 collective-permute-done.behind_ref
  123.8 4.1 %backward.1 = bf16[1024,768]{1,0:T(8,128)(2,1)S(1)} custom-call(s32[1]{0:T(128)} %bitcast.2.me_ref, bf16[1024,512]{1,0:T(8,128)(2,1)S(1)} %get-tuple-element.18.rows_ref, bf16[256,128]{1,0:T(8,128)(2,1)S(1)} %get-tuple-element.19.dup_ref, bf16[512,256]{1,0:T(8,128)(2,1)S(1)} %all_gather.16.pair_ref, bf16[272,256]{1,0:T(8,128)(2,1)S(1)} %collective-permute-done.behind_ref, ...), custom_call_target="tpu_custom_call" | custom-call | tf_op jit(solution)/shard_map/backward/pallas_call | solution.py:345
  127.9 48.9 %all_to_all.23 = bf16[128,8,768]{2,1,0:T(8,128)(2,1)S(1)} all-to-all(bf16[128,8,768]{2,1,0:T(8,128)(2,1)S(1)} %bitcast.10), channel_id=1, replica_groups=mesh['seq'=128,'head'=4] {'seq'}, dimensions={0} | all-to-all | bytes 3145728 | tf_op jit(solution)/shard_map/all_to_all | solution.py:360
  176.8 1.6 final.1
Async XLA Ops:
  101.6 22.2 %collective-permute-start = (bf16[272,256]{1,0:T(8,128)(2,1)S(1)}, bf16[272,256]{1,0:T(8,128)(2,1)S(1)}, u32[]{:S(2)}, u32[]{:S(2)}) collective-permute-start(bf16[272,256]{1,0:T(8,128)(2,1)S(1)} %get-tuple-element.21), channel_id=1, source_target_pairs={{4,0},{8,4},{12,8},{16,12},{20,16},{24,20},{28,24},{32,28},{36,32}... | collective-permute-start | bytes 417800 | tf_op jit(solution)/shard_map/ppermute | solution.py:378

commit v4 on v3

--- a/solution.py
+++ b/solution.py
@@ -195,7 +195,7 @@
     return ref[span * SPAN : (span + 1) * SPAN, unit * HEAD_DIM : (unit + 1) * HEAD_DIM]
 
 
-def forward_kernel(me_ref, rows_ref, dup_ref, pair_ref, table_ref, stats_ref):
+def forward_kernel(me_ref, rows_ref, dup_ref, pair_ref, table_ref, stats_ref, tile_ref):
     front = before_group((me_ref[0] & 1) == 1, dup_ref, pair_ref)
     for span in range(GROUP):
         q, g, k, v = (unit_of(rows_ref, span, unit) for unit in range(4))
@@ -215,12 +215,17 @@
             raised * dot_nt(v, g) + raised_front * dot_nt(v_front, g), axis=0, keepdims=True
         )
         here = slice(span * SPAN, (span + 1) * SPAN)
-        for kind, row in enumerate((highest + jnp.log(total), mixed / total)):
-            stats_ref[kind : kind + 1, here] = row
+        log_total = highest + jnp.log(total)
+        high = log_total.astype(BF16).astype(F32)
+        rows = (high, log_total - high, mixed / total)
+        for kind, row in enumerate(rows):
             for i in range(2):
-                at = kind * SLOTS + span * 2 + i
-                table_ref[at : at + 1, :] = row[:, i * LANES : (i + 1) * LANES]
+                at = kind * 2 * GROUP + span * 2 + i
+                tile_ref[at : at + 1, :] = row[:, i * LANES : (i + 1) * LANES]
+        stats_ref[0:1, here] = log_total
+        stats_ref[1:2, here] = rows[2]
     stats_ref[2:, :] = jnp.zeros((6, GROUP * SPAN), F32)
+    table_ref[...] = jnp.broadcast_to(tile_ref[...].astype(BF16)[None], table_ref.shape)
 
 
 def backward_kernel(
@@ -244,26 +249,23 @@
     behind_info = behind_ref[SPAN : SPAN + 8, :].astype(F32)
     far = jnp.concatenate([info_ref[0:1, :], behind_info[0:1]], axis=1).astype(I32)
     near = jnp.concatenate([info_ref[1:2, :], behind_info[1:2]], axis=1).astype(I32)
-    chosen = hot_rows(((far >> 3) & 15) * 16 + (far >> 7) * 8 + (far & 7))
+    chosen = hot_rows(far)
     keep = iota((LANES, far.shape[1]), 0) == near
 
-    def tile(turn, high, kind):
-        return pl.ds(pl.multiple_of(turn * 32 + high * 16 + kind * 8, 8), 8)
-
-    there = []
-    own = []
-    for kind in range(2):
-        tiles = [table_ref[:, tile(1 - turn, high, kind), :] for high in range(2)]
-        there.append(jnp.transpose(jnp.concatenate(tiles, axis=1).reshape(2 * LANES, LANES)))
-        next_tile = table_ref[group & 15, tile(turn, group >> 4, kind), :]
-        own.append(
-            jnp.concatenate([stats_ref[kind : kind + 1, :], next_tile[0:1], next_tile[1:2]], axis=1)
-        )
-    found = picked(jnp.concatenate(there, axis=0), chosen, dot)
+    there = table_ref[pl.ds(pl.multiple_of((1 - turn) * groups, groups), groups)].astype(F32)
+    there = [
+        jnp.transpose(there[:, kind * 8 : (kind + 1) * 8, :].reshape(groups * 8, LANES))
+        for kind in range(3)
+    ]
+    found = dot(jnp.concatenate(there, axis=0).astype(BF16), chosen)
     other = [
-        jnp.sum(
-            jnp.where(keep, found[kind * LANES : (kind + 1) * LANES], 0.0), axis=0, keepdims=True
-        )
+        jnp.sum(jnp.where(keep, values, 0.0), axis=0, keepdims=True)
+        for values in (found[:LANES] + found[LANES : 2 * LANES], found[2 * LANES :])
+    ]
+    tile = table_ref[turn * groups + group].astype(F32)
+    tiles = (tile[0:8] + tile[8:16], tile[16:24])
+    own = [
+        jnp.concatenate([stats_ref[kind : kind + 1, :], tiles[kind][0:1], tiles[kind][1:2]], axis=1)
         for kind in range(2)
     ]
     highest = jnp.maximum(own[0], other[0])
@@ -360,15 +362,18 @@
     return lax.all_to_all(block, "seq", split_axis=0, concat_axis=0, tiled=True)
 
 
-def gathered(block, members):
+def pair_gathered(block):
     n = lax.axis_size("seq")
-    taken = set()
-    groups = []
-    for first in range(n):
-        if first not in taken:
-            groups.append([first + offset for offset in members])
-            taken.update(groups[-1])
+    groups = [[i, i + 1] for i in range(0, n, 2)]
     return lax.all_gather(block, "seq", axis=0, tiled=True, axis_index_groups=groups)
+
+
+def head_exchanged(block):
+    n = lax.axis_size("seq")
+    groups = [list(range(i, i + n // 2)) for i in (0, n // 2)]
+    return lax.all_to_all(
+        block, "seq", split_axis=0, concat_axis=0, tiled=True, axis_index_groups=groups
+    )
 
 
 def from_next_group(block):
@@ -405,20 +410,19 @@
         (me, exchanged(send)),
     )
     behind = from_next_group(first)
-    pair = gathered(last, (0, 1))
+    pair = pair_gathered(last)
     table, stats = call(
         forward_kernel,
-        (shape(2 * SLOTS, LANES, dtype=F32), shape(8, places, dtype=F32)),
+        (shape(n // 2, 3 * 2 * GROUP, LANES), shape(8, places, dtype=F32)),
         "forward",
         (me, rows, dup, pair),
-    )
-    for members in ((0, n // 8), (0, n // 4), range(n // 8)):
-        table = gathered(table, members)
+        [pltpu.VMEM((3 * 2 * GROUP, LANES), F32)],
+    )
     grads = call(
         functools.partial(backward_kernel, n),
         shape(flat, 3 * HALVES * HEAD_DIM),
         "backward",
-        (me, rows, dup, pair, behind, info, stats, table.reshape(n // 8, 4 * 2 * SLOTS, LANES)),
+        (me, rows, dup, pair, behind, info, stats, head_exchanged(table)),
         [pltpu.VMEM((places, 3 * HEAD_DIM), BF16)],
     )
     return call(

time: 179 us -> 171 us (0.955)
  blocking collectives: 162 us -> 138 us
  waiting for transfers between devices: 0.01 us -> 11.9 us
  starting transfers between devices: 4.56 us -> 9.05 us
    all_gather x4 -> x1, blocking collectives: 27.3 us -> 2.3 us  [pair_gathered(): lax.all_gather(block, 'seq', axis=0, tiled=True, axis_index_groups=groups)]
    ppermute x1, waiting for transfers between devices: 0.01 us -> 8.86 us  [from_next_group(): return lax.ppermute(block, 'seq', route)]
    all_to_all x0 -> x1, starting transfers between devices: none -> 6.69 us  [head_exchanged(): lax.all_to_all(block, 'seq', split_axis=0, concat_axis=0, tiled=True, axi...]
    all_to_all x0 -> x1, waiting for transfers between devices: none -> 3.05 us  [head_exchanged(): lax.all_to_all(block, 'seq', split_axis=0, concat_axis=0, tiled=True, axi...]
    ppermute x1, starting transfers between devices: 4.56 us -> 2.36 us  [from_next_group(): return lax.ppermute(block, 'seq', route)]
  transfers between devices with their start and end apart: 1 -> 2, of which waited for: 0 -> 2; matrix products, arithmetic and copies ran while one was open for 0% -> 0% of each run, Pallas kernels for 0% -> 0%
where the time goes in v4:
time: 171 us
  blocking collectives  138 us (81%)
  waiting for transfers between devices  11.9 us (7%)
  Pallas kernels  10.7 us (6%)
  starting transfers between devices  9.05 us (5%)
    all_to_all x2, blocking collectives, exchanged(): return lax.all_to_all(block, 'seq', split_axis=0, concat_axis=0, tiled=True)  127 us
    pallas_call x5, Pallas kernels, call(): pl.pallas_call(kernel, out_shape=out, in_specs=[pl.BlockSpec(memory_space...  10.7 us
    ppermute x1, waiting for transfers between devices, from_next_group(): return lax.ppermute(block, 'seq', route)  8.86 us
    all_gather x1, blocking collectives, body(): placed = lax.all_gather(sorted_position, 'head', axis=0, tiled=True)  8.78 us
    all_to_all x1, starting transfers between devices, head_exchanged(): lax.all_to_all(block, 'seq', split_axis=0, concat_axis=0, tiled=True, axi...  6.69 us
  transfers between devices with their start and end apart: 2, of which 2 were waited for; matrix products, arithmetic and copies ran while one was open for 0% of the time, Pallas kernels for 0%

profile of v4, /device:TPU:1, one launch (start us, length us, event | category | flops | bytes accessed | tf_op | source)
XLA Modules:
  0.0 171.2 jit_solution(17115943851954280914)
XLA Ops:
  0.6 8.8 %all-gather = s32[4,2,64]{2,1,0:T(2,128)S(1)} all-gather(s32[1,2,64]{2,1,0:T(2,128)} %bitcast.12), channel_id=1, replica_groups=mesh['seq'=128,'head'=4] {'head'}, dimensions={0}, use_global_device_ids=true | all-gather | bytes 2560 | tf_op jit(solution)/shard_map/all_gather | solution.py:392
  9.4 1.2 pad_maximum_fusion.held_ref
  10.6 1.3 pack.1
  11.8 76.9 %all_to_all.27 = bf16[128,8,1152]{2,1,0:T(8,128)(2,1)S(1)} all-to-all(bf16[128,8,1152]{2,1,0:T(8,128)(2,1)S(1)} %bitcast.10), channel_id=1, replica_groups=mesh['seq'=128,'head'=4] {'seq'}, dimensions={0} | all-to-all | bytes 4718592 | tf_op jit(solution)/shard_map/all_to_all | solution.py:362
  88.8 2.2 %unpack.1 = (bf16[1024,512]{1,0:T(8,128)(2,1)S(1)}, bf16[256,128]{1,0:T(8,128)(2,1)S(1)}, bf16[256,256]{1,0:T(8,128)(2,1)S(1)}, bf16[272,256]{1,0:T(8,128)(2,1)S(1)}, f32[8,1024]{1,0:T(8,128)S(1)}) custom-call(s32[1]{0:T(128)} %bitcast.2.me_ref, bf16[1024,1152]{1,0:T(8,128)(2,1)S(1)} %bitcast.7), custom_call_target="tpu_custom_call" | custom-call | tf_op jit(solution)/shard_map/unpack/pallas_call | solution.py:347
  90.9 2.3 %all_gather.7.pair_ref = bf16[512,256]{1,0:T(8,128)(2,1)S(1)} all-gather(bf16[256,256]{1,0:T(8,128)(2,1)S(1)} %get-tuple-element.20), channel_id=1, replica_groups={{0,4},{8,12},{16,20},{24,28},{32,36},{40,44},{48,52},{56,60},{64,68},{7..., dimensions={0}, use_global_device_ids=true | all-gather | bytes 393216 | tf_op jit(solution)/shard_map/all_gather | solution.py:368
  93.2 1.8 %forward.1 = (bf16[64,24,128]{2,1,0:T(8,128)(2,1)}, f32[8,1024]{1,0:T(8,128)S(1)}) custom-call(s32[1]{0:T(128)} %bitcast.2.me_ref, bf16[1024,512]{1,0:T(8,128)(2,1)S(1)} %get-tuple-element.18.rows_ref, bf16[256,128]{1,0:T(8,128)(2,1)S(1)} %get-tuple-element.19.dup_ref, bf16[512,256]{1,0:T(8,128)(2,1)S(1)} %all_gather.7.pair_ref), custom_call_target="tpu_custom_call" | custom-call | tf_op jit(solution)/shard_map/forward/pallas_call | solution.py:347
  95.0 6.7 %all-to-all-start.1 = ((bf16[64,24,128]{2,1,0:T(8,128)(2,1)}), bf16[64,24,128]{2,1,0:T(8,128)(2,1)S(1)}, u32[]{:S(2)}, u32[]{:S(2)}) async-start(bf16[64,24,128]{2,1,0:T(8,128)(2,1)} %get-tuple-element.24), calls=%async_computation.1 | async-start | bytes 786432 | tf_op jit(solution)/shard_map/all_to_all | solution.py:374
  101.7 2.4 %collective-permute-start = (bf16[272,256]{1,0:T(8,128)(2,1)S(1)}, bf16[272,256]{1,0:T(8,128)(2,1)S(1)}, u32[]{:S(2)}, u32[]{:S(2)}) collective-permute-start(bf16[272,256]{1,0:T(8,128)(2,1)S(1)} %get-tuple-element.21), channel_id=1, source_target_pairs={{4,0},{8,4},{12,8},{16,12},{20,16},{24,20},{28,24},{32,28},{36,32}... | collective-permute-start | bytes 417800 | tf_op jit(solution)/shard_map/ppermute | solution.py:383
  104.1 8.9 %collective-permute-done.behind_ref = bf16[272,256]{1,0:T(8,128)(2,1)S(1)} collective-permute-done((bf16[272,256]{1,0:T(8,128)(2,1)S(1)}, bf16[272,256]{1,0:T(8,128)(2,1)S(1)}, u32[]{:S(2)}, u32[]{:S(2)}) %collective-permute-start) | collective-permute-done | bytes 139296 | tf_op jit(solution)/shard_map/ppermute | solution.py:383
  113.0 3.1 %all-to-all-done.1.table_ref = bf16[64,24,128]{2,1,0:T(8,128)(2,1)S(1)} async-done(((bf16[64,24,128]{2,1,0:T(8,128)(2,1)}), bf16[64,24,128]{2,1,0:T(8,128)(2,1)S(1)}, u32[]{:S(2)}, u32[]{:S(2)}) %all-to-all-start.1) | async-done | bytes 393248 | tf_op jit(solution)/shard_map/all_to_all | solution.py:374
  116.0 3.8 %backward.1 = bf16[1024,768]{1,0:T(8,128)(2,1)S(1)} custom-call(s32[1]{0:T(128)} %bitcast.2.me_ref, bf16[1024,512]{1,0:T(8,128)(2,1)S(1)} %get-tuple-element.18.rows_ref, bf16[256,128]{1,0:T(8,128)(2,1)S(1)} %get-tuple-element.19.dup_ref, bf16[512,256]{1,0:T(8,128)(2,1)S(1)} %all_gather.7.pair_ref, bf16[272,256]{1,0:T(8,128)(2,1)S(1)} %collective-permute-done.behind_ref, ...), custom_call_target="tpu_custom_call" | custom-call | tf_op jit(solution)/shard_map/backward/pallas_call | solution.py:347
  119.9 49.6 %all_to_all.28 = bf16[128,8,768]{2,1,0:T(8,128)(2,1)S(1)} all-to-all(bf16[128,8,768]{2,1,0:T(8,128)(2,1)S(1)} %bitcast.9), channel_id=1, replica_groups=mesh['seq'=128,'head'=4] {'seq'}, dimensions={0} | all-to-all | bytes 3145728 | tf_op jit(solution)/shard_map/all_to_all | solution.py:362
  169.5 1.6 final.1
Async XLA Ops:
  95.0 21.0 %all-to-all-start.1 = ((bf16[64,24,128]{2,1,0:T(8,128)(2,1)}), bf16[64,24,128]{2,1,0:T(8,128)(2,1)S(1)}, u32[]{:S(2)}, u32[]{:S(2)}) async-start(bf16[64,24,128]{2,1,0:T(8,128)(2,1)} %get-tuple-element.24), calls=%async_computation.1 | async-start | bytes 786432 | tf_op jit(solution)/shard_map/all_to_all | solution.py:374
  101.7 11.2 %collective-permute-start = (bf16[272,256]{1,0:T(8,128)(2,1)S(1)}, bf16[272,256]{1,0:T(8,128)(2,1)S(1)}, u32[]{:S(2)}, u32[]{:S(2)}) collective-permute-start(bf16[272,256]{1,0:T(8,128)(2,1)S(1)} %get-tuple-element.21), channel_id=1, source_target_pairs={{4,0},{8,4},{12,8},{16,12},{20,16},{24,20},{28,24},{32,28},{36,32}... | collective-permute-start | bytes 417800 | tf_op jit(solution)/shard_map/ppermute | solution.py:383

commit v5 on v4

--- a/solution.py
+++ b/solution.py
@@ -195,25 +195,25 @@
     return ref[span * SPAN : (span + 1) * SPAN, unit * HEAD_DIM : (unit + 1) * HEAD_DIM]
 
 
+def key_set(rows_ref, front, span):
+    if span == 0:
+        return [
+            jnp.concatenate([front[i], unit_of(rows_ref, 0, 2 + i)], axis=0) for i in range(2)
+        ]
+    rows = slice((span - 1) * SPAN, (span + 1) * SPAN)
+    return [rows_ref[rows, i * HEAD_DIM : (i + 1) * HEAD_DIM] for i in (2, 3)]
+
+
 def forward_kernel(me_ref, rows_ref, dup_ref, pair_ref, table_ref, stats_ref, tile_ref):
     front = before_group((me_ref[0] & 1) == 1, dup_ref, pair_ref)
     for span in range(GROUP):
-        q, g, k, v = (unit_of(rows_ref, span, unit) for unit in range(4))
-        if span == 0:
-            k_front, v_front = front
-        else:
-            k_front, v_front = unit_of(rows_ref, span - 1, 2), unit_of(rows_ref, span - 1, 3)
+        q, g = unit_of(rows_ref, span, 0), unit_of(rows_ref, span, 1)
+        k, v = key_set(rows_ref, front, span)
         score = dot_nt(k, q) * SCALE
-        score_front = dot_nt(k_front, q) * SCALE
-        highest = jnp.maximum(
-            jnp.max(score, axis=0, keepdims=True), jnp.max(score_front, axis=0, keepdims=True)
-        )
+        highest = jnp.max(score, axis=0, keepdims=True)
         raised = jnp.exp(score - highest)
-        raised_front = jnp.exp(score_front - highest)
-        total = jnp.sum(raised + raised_front, axis=0, keepdims=True)
-        mixed = jnp.sum(
-            raised * dot_nt(v, g) + raised_front * dot_nt(v_front, g), axis=0, keepdims=True
-        )
+        total = jnp.sum(raised, axis=0, keepdims=True)
+        mixed = jnp.sum(raised * dot_nt(v, g), axis=0, keepdims=True)
         here = slice(span * SPAN, (span + 1) * SPAN)
         log_total = highest + jnp.log(total)
         high = log_total.astype(BF16).astype(F32)
@@ -240,6 +240,7 @@
     table_ref,
     send_ref,
     grads_ref,
+    turned_ref,
 ):
     flat = n * SLOTS
     groups = n // GROUP
@@ -285,45 +286,51 @@
             grad.astype(BF16)
         )
 
+    front = before_group((me & 1) == 1, dup_ref, pair_ref)
+    keys = jnp.concatenate([front[0], rows_ref[:, 2 * HEAD_DIM : 3 * HEAD_DIM]], axis=0)
+    keys = jnp.transpose(keys)
     grad_k = None
     grad_v = None
     for span in range(GROUP):
-        q, g, k, v = (unit_of(rows_ref, span, unit) for unit in range(4))
+        q, g = unit_of(rows_ref, span, 0), unit_of(rows_ref, span, 1)
+        k, v = key_set(rows_ref, front, span)
         here = slice(span * SPAN, (span + 1) * SPAN)
-        if span == 0:
-            k_front, v_front = before_group((me & 1) == 1, dup_ref, pair_ref)
-        else:
-            k_front, v_front = unit_of(rows_ref, span - 1, 2), unit_of(rows_ref, span - 1, 3)
-        row = (own[0][:, here], shares[:, here], means[:, here])
-        weight, scaled = graded(k, v, q, g, *row)
-        weight_front, scaled_front = graded(k_front, v_front, q, g, *row)
-        put(span, 0, dot_tn(scaled, k) + dot_tn(scaled_front, k_front))
+        weight, scaled = graded(k, v, q, g, own[0][:, here], shares[:, here], means[:, here])
+        turned_ref[:, here] = dot(keys[:, span * SPAN : (span + 2) * SPAN], scaled).astype(BF16)
+        part_k = dot(scaled, q)
+        part_v = dot(weight, g)
         if span > 0:
-            put(span - 1, 1, grad_k + dot(scaled_front, q))
-            put(span - 1, 2, grad_v + dot(weight_front, g))
-        grad_k = dot(scaled, q)
-        grad_v = dot(weight, g)
+            put(span - 1, 0, grad_k + part_k[:SPAN])
+            put(span - 1, 1, grad_v + part_v[:SPAN])
+        grad_k = part_k[SPAN:]
+        grad_v = part_v[SPAN:]
     here = slice(GROUP * SPAN, (GROUP + 1) * SPAN)
     q, g = behind_ref[:SPAN, :HEAD_DIM], behind_ref[:SPAN, HEAD_DIM:]
+    k, v = unit_of(rows_ref, GROUP - 1, 2), unit_of(rows_ref, GROUP - 1, 3)
     weight, scaled = graded(k, v, q, g, own[0][:, here], shares[:, here], means[:, here])
-    put(GROUP - 1, 1, grad_k + dot(scaled, q))
-    put(GROUP - 1, 2, grad_v + dot(weight, g))
-    wide = 3 * HEAD_DIM
+    put(GROUP - 1, 0, grad_k + dot(scaled, q))
+    put(GROUP - 1, 1, grad_v + dot(weight, g))
     slot = (info_ref[2:3, :] * SLOTS + info_ref[3:4, :]).astype(I32)
     for half in range(HALVES):
         here = slice(half * 2 * SPAN, (half + 1) * 2 * SPAN)
         for start in range(0, flat, SPAN):
             at = slot[:, here]
             across = hot_rows(jnp.where((at >= start) & (at < start + SPAN), at - start, -1))
-            send_ref[start : start + SPAN, half * wide : (half + 1) * wide] = dot(
-                across, grads_ref[here, :]
-            ).astype(BF16)
+            grad_kv = dot(across, grads_ref[here, :])
+            grads = (
+                dot_nt(across, turned_ref[:, here]),
+                grad_kv[:, :HEAD_DIM],
+                grad_kv[:, HEAD_DIM:],
+            )
+            devices = slice(start // SLOTS, (start + SPAN) // SLOTS)
+            for unit, grad in enumerate(grads):
+                rows = slice((half * 3 + unit) * SLOTS, (half * 3 + unit + 1) * SLOTS)
+                send_ref[devices, rows, :] = grad.reshape(SPAN // SLOTS, SLOTS, HEAD_DIM).astype(BF16)
 
 
 def final_kernel(n, slots_ref, ret_ref, dq_ref, dk_ref, dv_ref):
     tall = n // GROUP * SLOTS
     both = ROUNDS * tall
-    wide = 3 * HEAD_DIM
     slots = jnp.transpose(slots_ref[...].astype(F32)).astype(I32)
     at = iota((slots.shape[0], tall), 1)
     chosen = []
@@ -333,13 +340,16 @@
             row = (slot >> 4) * SLOTS + (slot & 7)
             chosen.append(hot(at == jnp.where(((slot >> 3) & 1) == half, row, -1)))
     chosen = [jnp.concatenate(chosen[i * 2 : i * 2 + 2], axis=1) for i in range(HALVES)]
+    devices = both // SLOTS
     for head in range(dq_ref.shape[1] // HEAD_DIM):
-        rows = slice(head * both, (head + 1) * both)
-        total = dot(chosen[0], ret_ref[rows, :wide]) + dot(chosen[1], ret_ref[rows, wide:])
         for unit, ref in enumerate((dq_ref, dk_ref, dv_ref)):
-            ref[:, head * HEAD_DIM : (head + 1) * HEAD_DIM] = total[
-                :, unit * HEAD_DIM : (unit + 1) * HEAD_DIM
-            ].astype(BF16)
+            total = None
+            for half in range(HALVES):
+                rows = slice((half * 3 + unit) * SLOTS, (half * 3 + unit + 1) * SLOTS)
+                part = ret_ref[head * devices : (head + 1) * devices, rows, :]
+                part = dot(chosen[half], part.reshape(both, HEAD_DIM))
+                total = part if total is None else total + part
+            ref[:, head * HEAD_DIM : (head + 1) * HEAD_DIM] = total.astype(BF16)
 
 
 def call(kernel, out, name, args, scratch=()):
@@ -420,10 +430,10 @@
     )
     grads = call(
         functools.partial(backward_kernel, n),
-        shape(flat, 3 * HALVES * HEAD_DIM),
+        shape(n, 3 * HALVES * SLOTS, HEAD_DIM),
         "backward",
         (me, rows, dup, pair, behind, info, stats, head_exchanged(table)),
-        [pltpu.VMEM((places, 3 * HEAD_DIM), BF16)],
+        [pltpu.VMEM((places, 2 * HEAD_DIM), BF16), pltpu.VMEM((HEAD_DIM, places), BF16)],
     )
     return call(
         functools.partial(final_kernel, n),

time: 171 us -> 171 us (level)
  no operation moved by 1% of the time
where the time goes in v5:
time: 171 us
  blocking collectives  138 us (81%)
  waiting for transfers between devices  11.9 us (7%)
  Pallas kernels  10.7 us (6%)
  starting transfers between devices  9.05 us (5%)
    all_to_all x2, blocking collectives, exchanged(): return lax.all_to_all(block, 'seq', split_axis=0, concat_axis=0, tiled=True)  127 us
    pallas_call x5, Pallas kernels, call(): pl.pallas_call(kernel, out_shape=out, in_specs=[pl.BlockSpec(memory_space...  10.7 us
    ppermute x1, waiting for transfers between devices, from_next_group(): return lax.ppermute(block, 'seq', route)  8.86 us
    all_gather x1, blocking collectives, body(): placed = lax.all_gather(sorted_position, 'head', axis=0, tiled=True)  8.78 us
    all_to_all x1, starting transfers between devices, head_exchanged(): lax.all_to_all(block, 'seq', split_axis=0, concat_axis=0, tiled=True, axi...  6.69 us
  transfers between devices with their start and end apart: 2, of which 2 were waited for; matrix products, arithmetic and copies ran while one was open for 0% of the time, Pallas kernels for 0%

profile of v5, /device:TPU:1, one launch (start us, length us, event | category | flops | bytes accessed | tf_op | source)
XLA Modules:
  0.0 171.2 jit_solution(10378163843282176854)
XLA Ops:
  0.6 8.8 %all-gather = s32[4,2,64]{2,1,0:T(2,128)S(1)} all-gather(s32[1,2,64]{2,1,0:T(2,128)} %bitcast.8), channel_id=1, replica_groups=mesh['seq'=128,'head'=4] {'head'}, dimensions={0}, use_global_device_ids=true | all-gather | bytes 2560 | tf_op jit(solution)/shard_map/all_gather | solution.py:402
  9.4 1.2 pad_maximum_fusion.held_ref
  10.6 1.3 pack.1
  11.8 76.9 %all_to_all.21 = bf16[128,8,1152]{2,1,0:T(8,128)(2,1)S(1)} all-to-all(bf16[128,8,1152]{2,1,0:T(8,128)(2,1)S(1)} %bitcast.6), channel_id=1, replica_groups=mesh['seq'=128,'head'=4] {'seq'}, dimensions={0} | all-to-all | bytes 4718592 | tf_op jit(solution)/shard_map/all_to_all | solution.py:372
  88.8 2.2 %unpack.1 = (bf16[1024,512]{1,0:T(8,128)(2,1)S(1)}, bf16[256,128]{1,0:T(8,128)(2,1)S(1)}, bf16[256,256]{1,0:T(8,128)(2,1)S(1)}, bf16[272,256]{1,0:T(8,128)(2,1)S(1)}, f32[8,1024]{1,0:T(8,128)S(1)}) custom-call(s32[1]{0:T(128)} %bitcast.2.me_ref, bf16[1024,1152]{1,0:T(8,128)(2,1)S(1)} %bitcast.5), custom_call_target="tpu_custom_call" | custom-call | tf_op jit(solution)/shard_map/unpack/pallas_call | solution.py:357
  90.9 2.3 %all_gather.7.pair_ref = bf16[512,256]{1,0:T(8,128)(2,1)S(1)} all-gather(bf16[256,256]{1,0:T(8,128)(2,1)S(1)} %get-tuple-element.20), channel_id=1, replica_groups={{0,4},{8,12},{16,20},{24,28},{32,36},{40,44},{48,52},{56,60},{64,68},{7..., dimensions={0}, use_global_device_ids=true | all-gather | bytes 393216 | tf_op jit(solution)/shard_map/all_gather | solution.py:378
  93.2 1.9 %forward.1 = (bf16[64,24,128]{2,1,0:T(8,128)(2,1)}, f32[8,1024]{1,0:T(8,128)S(1)}) custom-call(s32[1]{0:T(128)} %bitcast.2.me_ref, bf16[1024,512]{1,0:T(8,128)(2,1)S(1)} %get-tuple-element.18.rows_ref, bf16[256,128]{1,0:T(8,128)(2,1)S(1)} %get-tuple-element.19.dup_ref, bf16[512,256]{1,0:T(8,128)(2,1)S(1)} %all_gather.7.pair_ref), custom_call_target="tpu_custom_call" | custom-call | tf_op jit(solution)/shard_map/forward/pallas_call | solution.py:357
  95.1 6.7 %all-to-all-start.1 = ((bf16[64,24,128]{2,1,0:T(8,128)(2,1)}), bf16[64,24,128]{2,1,0:T(8,128)(2,1)S(1)}, u32[]{:S(2)}, u32[]{:S(2)}) async-start(bf16[64,24,128]{2,1,0:T(8,128)(2,1)} %get-tuple-element.24), calls=%async_computation.1 | async-start | bytes 786432 | tf_op jit(solution)/shard_map/all_to_all | solution.py:384
  101.8 2.4 %collective-permute-start = (bf16[272,256]{1,0:T(8,128)(2,1)S(1)}, bf16[272,256]{1,0:T(8,128)(2,1)S(1)}, u32[]{:S(2)}, u32[]{:S(2)}) collective-permute-start(bf16[272,256]{1,0:T(8,128)(2,1)S(1)} %get-tuple-element.21), channel_id=1, source_target_pairs={{4,0},{8,4},{12,8},{16,12},{20,16},{24,20},{28,24},{32,28},{36,32}... | collective-permute-start | bytes 417800 | tf_op jit(solution)/shard_map/ppermute | solution.py:393
  104.2 8.9 %collective-permute-done.behind_ref = bf16[272,256]{1,0:T(8,128)(2,1)S(1)} collective-permute-done((bf16[272,256]{1,0:T(8,128)(2,1)S(1)}, bf16[272,256]{1,0:T(8,128)(2,1)S(1)}, u32[]{:S(2)}, u32[]{:S(2)}) %collective-permute-start) | collective-permute-done | bytes 139296 | tf_op jit(solution)/shard_map/ppermute | solution.py:393
  113.1 3.1 %all-to-all-done.1.table_ref = bf16[64,24,128]{2,1,0:T(8,128)(2,1)S(1)} async-done(((bf16[64,24,128]{2,1,0:T(8,128)(2,1)}), bf16[64,24,128]{2,1,0:T(8,128)(2,1)S(1)}, u32[]{:S(2)}, u32[]{:S(2)}) %all-to-all-start.1) | async-done | bytes 393248 | tf_op jit(solution)/shard_map/all_to_all | solution.py:384
  116.1 3.6 %backward.1 = bf16[128,48,128]{2,1,0:T(8,128)(2,1)S(1)} custom-call(s32[1]{0:T(128)} %bitcast.2.me_ref, bf16[1024,512]{1,0:T(8,128)(2,1)S(1)} %get-tuple-element.18.rows_ref, bf16[256,128]{1,0:T(8,128)(2,1)S(1)} %get-tuple-element.19.dup_ref, bf16[512,256]{1,0:T(8,128)(2,1)S(1)} %all_gather.7.pair_ref, bf16[272,256]{1,0:T(8,128)(2,1)S(1)} %collective-permute-done.behind_ref, ...), custom_call_target="tpu_custom_call" | custom-call | tf_op jit(solution)/shard_map/backward/pallas_call | solution.py:357
  119.7 49.6 %all_to_all.22.ret_ref = bf16[128,48,128]{2,1,0:T(8,128)(2,1)S(1)} all-to-all(bf16[128,48,128]{2,1,0:T(8,128)(2,1)S(1)} %backward.1), channel_id=1, replica_groups=mesh['seq'=128,'head'=4] {'seq'}, dimensions={0} | all-to-all | bytes 3145728 | tf_op jit(solution)/shard_map/all_to_all | solution.py:372
  169.4 1.8 %final.1 = (bf16[256,256]{1,0:T(8,128)(2,1)}, bf16[256,256]{1,0:T(8,128)(2,1)}, bf16[256,256]{1,0:T(8,128)(2,1)}) custom-call(s32[8,256]{1,0:T(8,128)S(1)} %get-tuple-element.14.slots_ref, bf16[128,48,128]{2,1,0:T(8,128)(2,1)S(1)} %all_to_all.22.ret_ref), custom_call_target="tpu_custom_call" | custom-call | tf_op jit(solution)/shard_map/final/pallas_call | solution.py:357
Async XLA Ops:
  95.1 21.0 %all-to-all-start.1 = ((bf16[64,24,128]{2,1,0:T(8,128)(2,1)}), bf16[64,24,128]{2,1,0:T(8,128)(2,1)S(1)}, u32[]{:S(2)}, u32[]{:S(2)}) async-start(bf16[64,24,128]{2,1,0:T(8,128)(2,1)} %get-tuple-element.24), calls=%async_computation.1 | async-start | bytes 786432 | tf_op jit(solution)/shard_map/all_to_all | solution.py:384
  101.8 11.2 %collective-permute-start = (bf16[272,256]{1,0:T(8,128)(2,1)S(1)}, bf16[272,256]{1,0:T(8,128)(2,1)S(1)}, u32[]{:S(2)}, u32[]{:S(2)}) collective-permute-start(bf16[272,256]{1,0:T(8,128)(2,1)S(1)} %get-tuple-element.21), channel_id=1, source_target_pairs={{4,0},{8,4},{12,8},{16,12},{20,16},{24,20},{28,24},{32,28},{36,32}... | collective-permute-start | bytes 417800 | tf_op jit(solution)/shard_map/ppermute | solution.py:393

commit v6 on v5

--- a/solution.py
+++ b/solution.py
@@ -310,27 +310,23 @@
     weight, scaled = graded(k, v, q, g, own[0][:, here], shares[:, here], means[:, here])
     put(GROUP - 1, 0, grad_k + dot(scaled, q))
     put(GROUP - 1, 1, grad_v + dot(weight, g))
+    wide = 3 * HEAD_DIM
     slot = (info_ref[2:3, :] * SLOTS + info_ref[3:4, :]).astype(I32)
     for half in range(HALVES):
         here = slice(half * 2 * SPAN, (half + 1) * 2 * SPAN)
         for start in range(0, flat, SPAN):
             at = slot[:, here]
             across = hot_rows(jnp.where((at >= start) & (at < start + SPAN), at - start, -1))
-            grad_kv = dot(across, grads_ref[here, :])
-            grads = (
-                dot_nt(across, turned_ref[:, here]),
-                grad_kv[:, :HEAD_DIM],
-                grad_kv[:, HEAD_DIM:],
-            )
-            devices = slice(start // SLOTS, (start + SPAN) // SLOTS)
-            for unit, grad in enumerate(grads):
-                rows = slice((half * 3 + unit) * SLOTS, (half * 3 + unit + 1) * SLOTS)
-                send_ref[devices, rows, :] = grad.reshape(SPAN // SLOTS, SLOTS, HEAD_DIM).astype(BF16)
+            rows = slice(start, start + SPAN)
+            middle = half * wide + HEAD_DIM
+            send_ref[rows, half * wide : middle] = dot_nt(across, turned_ref[:, here]).astype(BF16)
+            send_ref[rows, middle : (half + 1) * wide] = dot(across, grads_ref[here, :]).astype(BF16)
 
 
 def final_kernel(n, slots_ref, ret_ref, dq_ref, dk_ref, dv_ref):
     tall = n // GROUP * SLOTS
     both = ROUNDS * tall
+    wide = 3 * HEAD_DIM
     slots = jnp.transpose(slots_ref[...].astype(F32)).astype(I32)
     at = iota((slots.shape[0], tall), 1)
     chosen = []
@@ -340,16 +336,13 @@
             row = (slot >> 4) * SLOTS + (slot & 7)
             chosen.append(hot(at == jnp.where(((slot >> 3) & 1) == half, row, -1)))
     chosen = [jnp.concatenate(chosen[i * 2 : i * 2 + 2], axis=1) for i in range(HALVES)]
-    devices = both // SLOTS
     for head in range(dq_ref.shape[1] // HEAD_DIM):
+        rows = slice(head * both, (head + 1) * both)
+        total = dot(chosen[0], ret_ref[rows, :wide]) + dot(chosen[1], ret_ref[rows, wide:])
         for unit, ref in enumerate((dq_ref, dk_ref, dv_ref)):
-            total = None
-            for half in range(HALVES):
-                rows = slice((half * 3 + unit) * SLOTS, (half * 3 + unit + 1) * SLOTS)
-                part = ret_ref[head * devices : (head + 1) * devices, rows, :]
-                part = dot(chosen[half], part.reshape(both, HEAD_DIM))
-                total = part if total is None else total + part
-            ref[:, head * HEAD_DIM : (head + 1) * HEAD_DIM] = total.astype(BF16)
+            ref[:, head * HEAD_DIM : (head + 1) * HEAD_DIM] = total[
+                :, unit * HEAD_DIM : (unit + 1) * HEAD_DIM
+            ].astype(BF16)
 
 
 def call(kernel, out, name, args, scratch=()):
@@ -430,7 +423,7 @@
     )
     grads = call(
         functools.partial(backward_kernel, n),
-        shape(n, 3 * HALVES * SLOTS, HEAD_DIM),
+        shape(flat, 3 * HALVES * HEAD_DIM),
         "backward",
         (me, rows, dup, pair, behind, info, stats, head_exchanged(table)),
         [pltpu.VMEM((places, 2 * HEAD_DIM), BF16), pltpu.VMEM((HEAD_DIM, places), BF16)],

time: 171 us -> 171 us (level)
  no operation moved by 1% of the time
where the time goes in v6:
time: 171 us
  blocking collectives  138 us (81%)
  waiting for transfers between devices  11.9 us (7%)
  Pallas kernels  10.5 us (6%)
  starting transfers between devices  9.05 us (5%)
    all_to_all x2, blocking collectives, exchanged(): return lax.all_to_all(block, 'seq', split_axis=0, concat_axis=0, tiled=True)  127 us
    pallas_call x5, Pallas kernels, call(): pl.pallas_call(kernel, out_shape=out, in_specs=[pl.BlockSpec(memory_space...  10.5 us
    ppermute x1, waiting for transfers between devices, from_next_group(): return lax.ppermute(block, 'seq', route)  8.86 us
    all_gather x1, blocking collectives, body(): placed = lax.all_gather(sorted_position, 'head', axis=0, tiled=True)  8.78 us
    all_to_all x1, starting transfers between devices, head_exchanged(): lax.all_to_all(block, 'seq', split_axis=0, concat_axis=0, tiled=True, axi...  6.69 us
  transfers between devices with their start and end apart: 2, of which 2 were waited for; matrix products, arithmetic and copies ran while one was open for 0% of the time, Pallas kernels for 0%

profile of v6, /device:TPU:1, one launch (start us, length us, event | category | flops | bytes accessed | tf_op | source)
XLA Modules:
  0.0 171.0 jit_solution(10109703968024812619)
XLA Ops:
  0.6 8.8 %all-gather = s32[4,2,64]{2,1,0:T(2,128)S(1)} all-gather(s32[1,2,64]{2,1,0:T(2,128)} %bitcast.12), channel_id=1, replica_groups=mesh['seq'=128,'head'=4] {'head'}, dimensions={0}, use_global_device_ids=true | all-gather | bytes 2560 | tf_op jit(solution)/shard_map/all_gather | solution.py:395
  9.4 1.2 pad_maximum_fusion.held_ref
  10.6 1.3 pack.1
  11.8 76.9 %all_to_all.27 = bf16[128,8,1152]{2,1,0:T(8,128)(2,1)S(1)} all-to-all(bf16[128,8,1152]{2,1,0:T(8,128)(2,1)S(1)} %bitcast.10), channel_id=1, replica_groups=mesh['seq'=128,'head'=4] {'seq'}, dimensions={0} | all-to-all | bytes 4718592 | tf_op jit(solution)/shard_map/all_to_all | solution.py:365
  88.8 2.2 %unpack.1 = (bf16[1024,512]{1,0:T(8,128)(2,1)S(1)}, bf16[256,128]{1,0:T(8,128)(2,1)S(1)}, bf16[256,256]{1,0:T(8,128)(2,1)S(1)}, bf16[272,256]{1,0:T(8,128)(2,1)S(1)}, f32[8,1024]{1,0:T(8,128)S(1)}) custom-call(s32[1]{0:T(128)} %bitcast.2.me_ref, bf16[1024,1152]{1,0:T(8,128)(2,1)S(1)} %bitcast.7), custom_call_target="tpu_custom_call" | custom-call | tf_op jit(solution)/shard_map/unpack/pallas_call | solution.py:350
  90.9 2.3 %all_gather.7.pair_ref = bf16[512,256]{1,0:T(8,128)(2,1)S(1)} all-gather(bf16[256,256]{1,0:T(8,128)(2,1)S(1)} %get-tuple-element.20), channel_id=1, replica_groups={{0,4},{8,12},{16,20},{24,28},{32,36},{40,44},{48,52},{56,60},{64,68},{7..., dimensions={0}, use_global_device_ids=true | all-gather | bytes 393216 | tf_op jit(solution)/shard_map/all_gather | solution.py:371
  93.2 1.9 %forward.1 = (bf16[64,24,128]{2,1,0:T(8,128)(2,1)}, f32[8,1024]{1,0:T(8,128)S(1)}) custom-call(s32[1]{0:T(128)} %bitcast.2.me_ref, bf16[1024,512]{1,0:T(8,128)(2,1)S(1)} %get-tuple-element.18.rows_ref, bf16[256,128]{1,0:T(8,128)(2,1)S(1)} %get-tuple-element.19.dup_ref, bf16[512,256]{1,0:T(8,128)(2,1)S(1)} %all_gather.7.pair_ref), custom_call_target="tpu_custom_call" | custom-call | tf_op jit(solution)/shard_map/forward/pallas_call | solution.py:350
  95.1 6.7 %all-to-all-start.1 = ((bf16[64,24,128]{2,1,0:T(8,128)(2,1)}), bf16[64,24,128]{2,1,0:T(8,128)(2,1)S(1)}, u32[]{:S(2)}, u32[]{:S(2)}) async-start(bf16[64,24,128]{2,1,0:T(8,128)(2,1)} %get-tuple-element.24), calls=%async_computation.1 | async-start | bytes 786432 | tf_op jit(solution)/shard_map/all_to_all | solution.py:377
  101.8 2.4 %collective-permute-start = (bf16[272,256]{1,0:T(8,128)(2,1)S(1)}, bf16[272,256]{1,0:T(8,128)(2,1)S(1)}, u32[]{:S(2)}, u32[]{:S(2)}) collective-permute-start(bf16[272,256]{1,0:T(8,128)(2,1)S(1)} %get-tuple-element.21), channel_id=1, source_target_pairs={{4,0},{8,4},{12,8},{16,12},{20,16},{24,20},{28,24},{32,28},{36,32}... | collective-permute-start | bytes 417800 | tf_op jit(solution)/shard_map/ppermute | solution.py:386
  104.2 8.9 %collective-permute-done.behind_ref = bf16[272,256]{1,0:T(8,128)(2,1)S(1)} collective-permute-done((bf16[272,256]{1,0:T(8,128)(2,1)S(1)}, bf16[272,256]{1,0:T(8,128)(2,1)S(1)}, u32[]{:S(2)}, u32[]{:S(2)}) %collective-permute-start) | collective-permute-done | bytes 139296 | tf_op jit(solution)/shard_map/ppermute | solution.py:386
  113.1 3.1 %all-to-all-done.1.table_ref = bf16[64,24,128]{2,1,0:T(8,128)(2,1)S(1)} async-done(((bf16[64,24,128]{2,1,0:T(8,128)(2,1)}), bf16[64,24,128]{2,1,0:T(8,128)(2,1)S(1)}, u32[]{:S(2)}, u32[]{:S(2)}) %all-to-all-start.1) | async-done | bytes 393248 | tf_op jit(solution)/shard_map/all_to_all | solution.py:377
  116.1 3.6 %backward.1 = bf16[1024,768]{1,0:T(8,128)(2,1)S(1)} custom-call(s32[1]{0:T(128)} %bitcast.2.me_ref, bf16[1024,512]{1,0:T(8,128)(2,1)S(1)} %get-tuple-element.18.rows_ref, bf16[256,128]{1,0:T(8,128)(2,1)S(1)} %get-tuple-element.19.dup_ref, bf16[512,256]{1,0:T(8,128)(2,1)S(1)} %all_gather.7.pair_ref, bf16[272,256]{1,0:T(8,128)(2,1)S(1)} %collective-permute-done.behind_ref, ...), custom_call_target="tpu_custom_call" | custom-call | tf_op jit(solution)/shard_map/backward/pallas_call | solution.py:350
  119.7 49.6 %all_to_all.28 = bf16[128,8,768]{2,1,0:T(8,128)(2,1)S(1)} all-to-all(bf16[128,8,768]{2,1,0:T(8,128)(2,1)S(1)} %bitcast.9), channel_id=1, replica_groups=mesh['seq'=128,'head'=4] {'seq'}, dimensions={0} | all-to-all | bytes 3145728 | tf_op jit(solution)/shard_map/all_to_all | solution.py:365
  169.3 1.6 final.1
Async XLA Ops:
  95.1 21.0 %all-to-all-start.1 = ((bf16[64,24,128]{2,1,0:T(8,128)(2,1)}), bf16[64,24,128]{2,1,0:T(8,128)(2,1)S(1)}, u32[]{:S(2)}, u32[]{:S(2)}) async-start(bf16[64,24,128]{2,1,0:T(8,128)(2,1)} %get-tuple-element.24), calls=%async_computation.1 | async-start | bytes 786432 | tf_op jit(solution)/shard_map/all_to_all | solution.py:377
  101.8 11.2 %collective-permute-start = (bf16[272,256]{1,0:T(8,128)(2,1)S(1)}, bf16[272,256]{1,0:T(8,128)(2,1)S(1)}, u32[]{:S(2)}, u32[]{:S(2)}) collective-permute-start(bf16[272,256]{1,0:T(8,128)(2,1)S(1)} %get-tuple-element.21), channel_id=1, source_target_pairs={{4,0},{8,4},{12,8},{16,12},{20,16},{24,20},{28,24},{32,28},{36,32}... | collective-permute-start | bytes 417800 | tf_op jit(solution)/shard_map/ppermute | solution.py:386
